TPU v7x, 256 devices: a whole 4x4x8 slice. The times are simulated.
256 devices in a mesh: dp: 8 (over y, z_hi), tensor: 32 (over x, z_lo, core).
Axes of the slice: x: 4, y: 4, z: 8 (z_hi: 2, z_lo: 4; z = z_hi * 4 + z_lo), core: 2. Of those that a mesh axis runs over, the one named last changes fastest.
Arguments:
- tokens: bfloat16 [1024, 16384], P('dp', 'tensor'), may hold values from -6 to 6
- mixed: bfloat16 [1024, 16384], P('dp', 'tensor'), may hold values from -6 to 6
- angles: float32 [4, 5, 8192], replicated, may hold values from -1 to 1
- q_packed: float32 [4096, 8192], P('tensor'), may hold values from 0 to 65535, as said below
- q_scale: bfloat16 [256, 8192], P('tensor'), may hold values from 0.0007972717 to 0.003189087
- k_packed: float32 [4096, 1024], P('tensor'), may hold values from 0 to 65535, as said below
- k_scale: bfloat16 [256, 1024], P('tensor'), may hold values from 0.0007972717 to 0.003189087
- v_packed: float32 [4096, 1024], P('tensor'), may hold values from 0 to 65535, as said below
- v_scale: bfloat16 [256, 1024], P('tensor'), may hold values from 0.0007972717 to 0.003189087
- o_packed: float32 [4096, 8192], P('tensor'), may hold values from 0 to 65535, as said below
- o_scale: bfloat16 [256, 8192], P('tensor'), may hold values from 0.0007972717 to 0.003189087
- q_cot: bfloat16 [1024, 8192], P('dp', 'tensor'), may hold values from -1.5 to 1.5
- k_cot: bfloat16 [1024, 1024], P('dp', 'tensor'), may hold values from -6 to 6
- v_cot: bfloat16 [1024, 1024], P('dp', 'tensor'), may hold values from -6 to 6
- o_cot: bfloat16 [1024, 8192], P('dp', 'tensor'), may hold values from -1.5 to 1.5
Outputs:
- q_out: bfloat16 [1024, 8192], P('dp', 'tensor')
- k_out: bfloat16 [1024, 1024], P('dp', 'tensor')
- v_out: bfloat16 [1024, 1024], P('dp', 'tensor')
- o_out: bfloat16 [1024, 8192], P('dp', 'tensor')
- token_grad: bfloat16 [1024, 16384], P('dp', 'tensor')
- mixed_grad: bfloat16 [1024, 16384], P('dp', 'tensor')
- angle_grad: float32 [4, 5, 16384], P(None, None, 'tensor')
Inputs may be any that keep to these rules, and one draw needn't show every extreme that they name: `q_packed`: each entry is a whole number; it holds the 4-bit codes of four consecutive input rows, row 4 w + i in base-16 digit i of entry w. `k_packed`: packed as q_packed. `v_packed`: packed as q_packed. `o_packed`: packed as q_packed.
All inputs are finite; a program needn't handle non-finite values.
Results may differ from a plain program's by a relative error of at most 0.034.
Values may be sent and summed in bfloat16 or wider, within the bound.
A program may use at most 320 MiB of HBM per device.

v0:
```python
import jax
import jax.numpy as jnp
from jax import lax
from jax.sharding import PartitionSpec as P

D = 16384
SECTIONS = 5


def from_partner(value, axis, distance):
    return lax.ppermute(value, axis, [(i, i ^ 1 << distance) for i in range(lax.axis_size(axis))])


def shortened(value):

    def short(part):
        return part.astype(jnp.bfloat16) if part.dtype == jnp.float32 else part

    return jax.tree.map(short, value)


def dequantize(packed, scale):
    word_rows = packed.shape[0]
    columns = packed.shape[1]
    grouped = packed.reshape(scale.shape[0], word_rows // scale.shape[0], columns)
    spread = scale.astype(jnp.float32)[:, None, :]
    planes = []
    for factor in (1.0, 0.0625, 0.00390625, 0.000244140625):
        scaled = grouped * factor
        digit = jnp.floor(scaled) - 16.0 * jnp.floor(scaled * 0.0625)
        planes.append(((digit - 7.5) * spread).reshape(word_rows, columns).astype(jnp.bfloat16))
    return jnp.stack(planes)


def rotation(angle):
    square = angle * angle
    denominator = 1.0 + square
    return ((1.0 - square) / denominator, 2.0 * angle / denominator)


def rotation_slope(angle):
    square = angle * angle
    denominator = (1.0 + square) * (1.0 + square)
    return (-4.0 * angle / denominator, 2.0 * (1.0 - square) / denominator)


def pair_index(channels, section_bit):
    upper_part = jnp.left_shift(jnp.right_shift(channels, section_bit + 1), section_bit)
    return jnp.bitwise_or(upper_part, jnp.bitwise_and(channels, (1 << section_bit) - 1))


def parity(channels, section_bit):
    upper_flag = jnp.bitwise_and(jnp.right_shift(channels, section_bit), 1) == 1
    return jnp.where(upper_flag, 1.0, -1.0).astype(jnp.float32)


def widen(values):
    return jnp.concatenate([values[:1], values[:1], values[:1], values[1:]], axis=0)


def forward_sections(stacked, angles, channels, fetch):
    log_width = D.bit_length() - 1
    current = stacked
    stored = []
    for section_num in range(SECTIONS):
        section_bit = log_width - 1 - section_num
        partner = fetch(current, section_bit)
        if section_num == 0:
            current = widen(current)
            partner = widen(partner)
        stored.append((current, partner))
        angle = jnp.take(angles[:, section_num], pair_index(channels, section_bit), axis=1)[
            :, None, :
        ]
        cosine, sine = rotation(angle)
        signs = parity(channels, section_bit)
        mixed_up = cosine * current.astype(jnp.float32) + signs * sine * partner.astype(jnp.float32)
        current = mixed_up.astype(jnp.bfloat16)
    return (current, stored)


def backward_sections(cotangent, stored, angles, channels, fetch):
    log_width = D.bit_length() - 1
    shares = []
    for section_num in reversed(range(SECTIONS)):
        section_bit = log_width - 1 - section_num
        state, partner = stored[section_num]
        cot_partner = fetch(cotangent, section_bit)
        angle = jnp.take(angles[:, section_num], pair_index(channels, section_bit), axis=1)[
            :, None, :
        ]
        cosine, sine = rotation(angle)
        cos_slope, sin_slope = rotation_slope(angle)
        signs = parity(channels, section_bit)
        grad_own = cotangent.astype(jnp.float32)
        grad_other = cot_partner.astype(jnp.float32)
        own_state = state.astype(jnp.float32)
        other_state = partner.astype(jnp.float32)
        direct = jnp.sum(grad_own * own_state + grad_other * other_state, axis=1)
        crossed = jnp.sum(grad_own * other_state - grad_other * own_state, axis=1)
        shares.insert(0, direct * cos_slope[:, 0] + signs * crossed * sin_slope[:, 0])
        result = cosine * grad_own - signs * sine * grad_other
        cotangent = result if section_num == 0 else result.astype(jnp.bfloat16)
    return (cotangent, jnp.stack(shares, axis=1))


def project_rows(activation, planes):
    tok_rows = activation.shape[0]
    split_rows = activation.reshape(tok_rows, planes.shape[1], 4).transpose(2, 0, 1)
    return lax.dot_general(
        split_rows, planes, (((0, 2), (0, 1)), ((), ())), preferred_element_type=jnp.float32
    )


def contract(piece, planes):
    return lax.dot_general(
        piece, planes, (((1,), (2,)), ((), ())), preferred_element_type=jnp.float32
    )


def to_channels(carried):
    tok_rows = carried.shape[0]
    return carried.transpose(0, 2, 1).reshape(tok_rows, -1)


def shards(
    tokens,
    mixed,
    angles,
    q_packed,
    q_scale,
    k_packed,
    k_scale,
    v_packed,
    v_scale,
    o_packed,
    o_scale,
    q_cot,
    k_cot,
    v_cot,
    o_cot,
):
    slab_width = tokens.shape[1]
    weights = [
        dequantize(q_packed, q_scale),
        dequantize(k_packed, k_scale),
        dequantize(v_packed, v_scale),
        dequantize(o_packed, o_scale),
    ]
    stacked = jnp.stack([tokens, mixed])
    channels = lax.axis_index("tensor") * slab_width + jnp.arange(slab_width, dtype=jnp.int32)
    local_bits = slab_width.bit_length() - 1

    def fetch_states(values, section_bit):
        return from_partner(values, "tensor", section_bit - local_bits)

    rotated, stored = forward_sections(stacked, angles, channels, fetch_states)
    partials = tuple(
        (project_rows(rotated[chain_num], weights[chain_num]) for chain_num in range(4))
    )
    q_sum, k_sum, v_sum, o_sum = jax.tree.map(
        lambda part: part.astype(jnp.float32),
        lax.psum_scatter(shortened(partials), "tensor", scatter_dimension=1, tiled=True),
    )
    pieces = (
        lax.all_gather(q_cot, "tensor", axis=1, tiled=True),
        lax.all_gather(o_cot, "tensor", axis=1, tiled=True),
    )
    q_cols = weights[0]
    o_cols = weights[3]
    q_back = contract(pieces[0], q_cols)
    o_back = contract(pieces[1], o_cols)
    pieces = (
        lax.all_gather(k_cot, "tensor", axis=1, tiled=True),
        lax.all_gather(v_cot, "tensor", axis=1, tiled=True),
    )
    k_cols = weights[1]
    v_cols = weights[2]
    k_back = contract(pieces[0], k_cols)
    v_back = contract(pieces[1], v_cols)
    backs = jnp.stack(
        [to_channels(q_back), to_channels(k_back), to_channels(v_back), to_channels(o_back)]
    ).astype(jnp.bfloat16)

    def fetch_grads(values, section_bit):
        return from_partner(values, "tensor", section_bit - local_bits)

    input_grads, angle_local = backward_sections(backs, stored, angles, channels, fetch_grads)
    grads_local = jnp.stack(
        [input_grads[0] + input_grads[1] + input_grads[2], input_grads[3]]
    ).astype(jnp.bfloat16)
    angle_grad = lax.psum(angle_local.astype(jnp.bfloat16), "dp").astype(jnp.float32)
    return (
        q_sum.astype(jnp.bfloat16),
        k_sum.astype(jnp.bfloat16),
        v_sum.astype(jnp.bfloat16),
        o_sum.astype(jnp.bfloat16),
        grads_local[0],
        grads_local[1],
        angle_grad,
    )


def solution(mesh):
    in_specs = (
        P("dp", "tensor"),
        P("dp", "tensor"),
        P(),
        P("tensor", None),
        P("tensor", None),
        P("tensor", None),
        P("tensor", None),
        P("tensor", None),
        P("tensor", None),
        P("tensor", None),
        P("tensor", None),
        P("dp", "tensor"),
        P("dp", "tensor"),
        P("dp", "tensor"),
        P("dp", "tensor"),
    )
    out_specs = (
        P("dp", "tensor"),
        P("dp", "tensor"),
        P("dp", "tensor"),
        P("dp", "tensor"),
        P("dp", "tensor"),
        P("dp", "tensor"),
        P(None, None, "tensor"),
    )
    return jax.shard_map(shards, mesh=mesh, in_specs=in_specs, out_specs=out_specs, check_vma=False)
```

profile of v0, /device:TPU:1, one launch (start us, length us, event | category | flops | bytes accessed | tf_op | source)
XLA Modules:
  0.0 792.6 jit_solution(3499288875401270969)
XLA Ops:
  10.8 3.6 collective-permute-start
  15.6 47.8 %all_gather.13 = bf16[128,1024]{0,1:T(8,128)(2,1)} all-gather(bf16[128,32]{0,1:T(8,128)(2,1)} %param.29), channel_id=1, replica_groups=mesh['dp'=8,'tensor'=32] {'tensor'}, dimensions={1}, use_global_device_ids=true | all-gather | bytes 270336 | tf_op jit(solution)/shard_map/all_gather | solution.py:174
  63.4 39.2 %all_gather.14 = bf16[128,1024]{0,1:T(8,128)(2,1)S(1)} all-gather(bf16[128,32]{0,1:T(8,128)(2,1)} %param.30), channel_id=1, replica_groups=mesh['dp'=8,'tensor'=32] {'tensor'}, dimensions={1}, use_global_device_ids=true | all-gather | bytes 270336 | tf_op jit(solution)/shard_map/all_gather | solution.py:175
  123.4 3.3 gather_fusion.4
  133.9 8.6 %collective-permute-done.1 = bf16[4,128,512]{1,2,0:T(8,128)(2,1)S(1)} collective-permute-done((bf16[4,128,512]{1,2,0:T(8,128)(2,1)S(1)}, bf16[4,128,512]{1,2,0:T(8,128)(2,1)S(1)}, u32[]{:S(2)}, u32[]{:S(2)}) %collective-permute-start.1) | collective-permute-done | bytes 524320 | tf_op jit(solution)/shard_map/ppermute | solution.py:11
  148.1 7.2 fusion.6
  155.4 5.7 fusion.2
  161.1 8.7 %collective-permute-done.2 = bf16[4,128,512]{1,2,0:T(8,128)(2,1)S(1)} collective-permute-done((bf16[4,128,512]{1,2,0:T(8,128)(2,1)S(1)}, bf16[4,128,512]{1,2,0:T(8,128)(2,1)S(1)}, u32[]{:S(2)}, u32[]{:S(2)}) %collective-permute-start.2) | collective-permute-done | bytes 524320 | tf_op jit(solution)/shard_map/ppermute | solution.py:11
  171.3 12.3 %collective-permute-done.3 = bf16[4,128,512]{1,2,0:T(8,128)(2,1)S(1)} collective-permute-done((bf16[4,128,512]{1,2,0:T(8,128)(2,1)S(1)}, bf16[4,128,512]{1,2,0:T(8,128)(2,1)S(1)}, u32[]{:S(2)}, u32[]{:S(2)}) %collective-permute-start.3) | collective-permute-done | bytes 524320 | tf_op jit(solution)/shard_map/ppermute | solution.py:11
  185.7 6.0 fusion.24
  192.5 6.1 fusion.27
  200.2 4.0 gather_fusion
  206.6 3.7 fusion.43
  215.9 5.3 fusion.1
  221.5 5.3 fusion
  226.9 8.1 %collective-permute-done.6 = bf16[4,128,512]{1,2,0:T(8,128)(2,1)} collective-permute-done((bf16[4,128,512]{1,2,0:T(8,128)(2,1)S(1)}, bf16[4,128,512]{1,2,0:T(8,128)(2,1)}, u32[]{:S(2)}, u32[]{:S(2)}) %collective-permute-start.6) | collective-permute-done | bytes 524320 | tf_op jit(solution)/shard_map/ppermute | solution.py:11
  237.6 26.3 %collective-permute-done.7 = bf16[4,128,512]{1,2,0:T(8,128)(2,1)S(1)} collective-permute-done((bf16[4,128,512]{1,2,0:T(8,128)(2,1)S(1)}, bf16[4,128,512]{1,2,0:T(8,128)(2,1)S(1)}, u32[]{:S(2)}, u32[]{:S(2)}) %collective-permute-start.7) | collective-permute-done | bytes 524320 | tf_op jit(solution)/shard_map/ppermute | solution.py:11
  265.7 12.8 %collective-permute-done.8 = bf16[4,128,512]{1,2,0:T(8,128)(2,1)S(1)} collective-permute-done((bf16[4,128,512]{1,2,0:T(8,128)(2,1)S(1)}, bf16[4,128,512]{1,2,0:T(8,128)(2,1)S(1)}, u32[]{:S(2)}, u32[]{:S(2)}) %collective-permute-start.8) | collective-permute-done | bytes 524320 | tf_op jit(solution)/shard_map/ppermute | solution.py:11
  280.7 14.0 %collective-permute-done.9 = bf16[4,128,512]{1,2,0:T(8,128)(2,1)S(1)} collective-permute-done((bf16[4,128,512]{1,2,0:T(8,128)(2,1)S(1)}, bf16[4,128,512]{1,2,0:T(8,128)(2,1)S(1)}, u32[]{:S(2)}, u32[]{:S(2)}) %collective-permute-start.9) | collective-permute-done | bytes 524320 | tf_op jit(solution)/shard_map/ppermute | solution.py:11
  296.4 45.4 %psum.7 = bf16[4,5,512]{2,0,1:T(4,128)(2,1)S(1)} all-reduce(bf16[4,5,512]{2,0,1:T(4,128)(2,1)S(1)} %constant_dynamic-update-slice_fusion), channel_id=1, replica_groups=mesh['dp'=8,'tensor'=32] {'dp'}, use_global_device_ids=true, to_apply=%region_14.16 | all-reduce | flops 10240 | bytes 40960 | tf_op jit(solution)/shard_map/psum | solution.py:192
  344.1 6.4 reduce-scatter.9.cloned.1.call-done
  350.4 142.5 %reduce-scatter.7.cloned.1.call-done = bf16[128,32]{0,1:T(8,128)(2,1)} async-done(((bf16[128,1024]{0,1:T(8,128)(2,1)}), bf16[128,32]{0,1:T(8,128)(2,1)}) %reduce-scatter.7.cloned.1.call-update) | async-done | bytes 8208 | tf_op jit(solution)/shard_map/reduce_scatter | solution.py:163
  493.0 146.0 %reduce-scatter.11.cloned.1.call-done = bf16[128,256]{1,0:T(8,128)(2,1)} async-done(((bf16[128,8192]{1,0:T(8,128)(2,1)}), bf16[128,256]{1,0:T(8,128)(2,1)}) %reduce-scatter.11.cloned.1.call-update) | async-done | bytes 65552 | tf_op jit(solution)/shard_map/reduce_scatter | solution.py:163
  639.0 146.7 %reduce-scatter.5.cloned.1.call-done = bf16[128,256]{1,0:T(8,128)(2,1)} async-done(((bf16[128,8192]{1,0:T(8,128)(2,1)}), bf16[128,256]{1,0:T(8,128)(2,1)}) %reduce-scatter.5.cloned.1.call-update) | async-done | bytes 65552 | tf_op jit(solution)/shard_map/reduce_scatter | solution.py:163
  (239 shorter events, 62.1 us)
Async XLA Ops:
  7.2 97.7 %copy-start.6 = (f32[128,1024]{1,0:T(8,128)S(1)}, f32[128,1024]{1,0:T(8,128)}, u32[]{:S(2)}) copy-start(f32[128,1024]{1,0:T(8,128)} %param.24) | copy-start | bytes 1572868
  7.2 97.9 %copy-start.51 = (bf16[8,1024]{1,0:T(8,128)(2,1)S(1)}, bf16[8,1024]{1,0:T(8,128)(2,1)}, u32[]{:S(2)}) copy-start(bf16[8,1024]{1,0:T(8,128)(2,1)} %param.25) | copy-start | bytes 49156
  7.2 178.5 %all-gather.5.cloned.1.call-start = ((), (), s32[]{:S(2)}) async-start(), calls=%async_computation.9 | async-start | bytes 2162688 | tf_op jit(solution)/shard_map/all_gather | solution.py:167
  7.9 184.6 %all-gather.3.cloned.1.call-start = ((), (), s32[]{:S(2)}) async-start(), calls=%async_computation.8 | async-start | bytes 2162688 | tf_op jit(solution)/shard_map/all_gather | solution.py:166
  10.8 116.1 %collective-permute-start = (bf16[2,128,512]{1,2,0:T(8,128)(2,1)}, bf16[2,128,512]{1,2,0:T(8,128)(2,1)S(1)}, u32[]{:S(2)}, u32[]{:S(2)}) collective-permute-start(bf16[2,128,512]{1,2,0:T(8,128)(2,1)} %pad_maximum_fusion.19), channel_id=1, source_target_pairs={{0,16},{1,17},{2,18},{3,19},{4,20},{5,21},{6,22},{7,23},{8,24},{9,... | collective-permute-start | bytes 786440 | tf_op jit(solution)/shard_map/ppermute | solution.py:11
  14.4 336.1 %reduce-scatter.9.cloned.1.call-start = ((), (), s32[]{:S(2)}) async-start(), calls=%async_computation.6 | async-start | bytes 270336 | tf_op jit(solution)/shard_map/reduce_scatter | solution.py:163
  127.6 14.9 %collective-permute-start.1 = (bf16[4,128,512]{1,2,0:T(8,128)(2,1)S(1)}, bf16[4,128,512]{1,2,0:T(8,128)(2,1)S(1)}, u32[]{:S(2)}, u32[]{:S(2)}) collective-permute-start(bf16[4,128,512]{1,2,0:T(8,128)(2,1)S(1)} %fusion.31), channel_id=1, source_target_pairs={{0,8},{1,9},{2,10},{3,11},{4,12},{5,13},{6,14},{7,15},{8,0},{9,1},... | collective-permute-start | bytes 1572872 | tf_op jit(solution)/shard_map/ppermute | solution.py:11
  143.9 26.0 %collective-permute-start.2 = (bf16[4,128,512]{1,2,0:T(8,128)(2,1)S(1)}, bf16[4,128,512]{1,2,0:T(8,128)(2,1)S(1)}, u32[]{:S(2)}, u32[]{:S(2)}) collective-permute-start(bf16[4,128,512]{1,2,0:T(8,128)(2,1)S(1)} %fusion.33), channel_id=1, source_target_pairs={{0,4},{1,5},{2,6},{3,7},{4,0},{5,1},{6,2},{7,3},{8,12},{9,13},{10,... | collective-permute-start | bytes 1572872 | tf_op jit(solution)/shard_map/ppermute | solution.py:11
  170.5 13.1 %collective-permute-start.3 = (bf16[4,128,512]{1,2,0:T(8,128)(2,1)S(1)}, bf16[4,128,512]{1,2,0:T(8,128)(2,1)S(1)}, u32[]{:S(2)}, u32[]{:S(2)}) collective-permute-start(bf16[4,128,512]{1,2,0:T(8,128)(2,1)S(1)} %fusion.35), channel_id=1, source_target_pairs={{0,2},{1,3},{2,0},{3,1},{4,6},{5,7},{6,4},{7,5},{8,10},{9,11},{10,... | collective-permute-start | bytes 1572872 | tf_op jit(solution)/shard_map/ppermute | solution.py:11
  184.3 22.3 %collective-permute-start.4 = (bf16[4,128,512]{1,2,0:T(8,128)(2,1)S(1)}, bf16[4,128,512]{1,2,0:T(8,128)(2,1)}, u32[]{:S(2)}, u32[]{:S(2)}) collective-permute-start(bf16[4,128,512]{1,2,0:T(8,128)(2,1)S(1)} %fusion.37), channel_id=1, source_target_pairs={{0,1},{1,0},{2,3},{3,2},{4,5},{5,4},{6,7},{7,6},{8,9},{9,8},{10,11... | collective-permute-start | bytes 1572872 | tf_op jit(solution)/shard_map/ppermute | solution.py:11
  199.6 7.1 collective-permute-start.5
  212.9 280.1 %reduce-scatter.7.cloned.1.call-start = ((), (), s32[]{:S(2)}) async-start(), calls=%async_computation.5 | async-start | bytes 270336 | tf_op jit(solution)/shard_map/reduce_scatter | solution.py:163
  215.6 423.4 %reduce-scatter.11.cloned.1.call-start = ((), (), s32[]{:S(2)}) async-start(), calls=%async_computation.7 | async-start | bytes 2162688 | tf_op jit(solution)/shard_map/reduce_scatter | solution.py:163
  221.2 564.5 %reduce-scatter.5.cloned.1.call-start = ((), (), s32[]{:S(2)}) async-start(), calls=%async_computation.4 | async-start | bytes 2162688 | tf_op jit(solution)/shard_map/reduce_scatter | solution.py:163
  221.4 13.6 %collective-permute-start.6 = (bf16[4,128,512]{1,2,0:T(8,128)(2,1)S(1)}, bf16[4,128,512]{1,2,0:T(8,128)(2,1)}, u32[]{:S(2)}, u32[]{:S(2)}) collective-permute-start(bf16[4,128,512]{1,2,0:T(8,128)(2,1)S(1)} %copy-done.1), channel_id=1, source_target_pairs={{0,2},{1,3},{2,0},{3,1},{4,6},{5,7},{6,4},{7,5},{8,10},{9,11},{10,... | collective-permute-start | bytes 1572872 | tf_op jit(solution)/shard_map/ppermute | solution.py:11
  237.4 58.8 %copy-start.29 = (f32[512,4]{0,1:T(4,128)S(1)}, f32[512,4]{0,1:T(4,128)}, u32[]{:S(2)}) copy-start(f32[512,4]{0,1:T(4,128)} %copy.185) | copy-start | bytes 24580
  237.4 58.9 %copy-start.30 = (f32[512,4]{0,1:T(4,128)S(1)}, f32[512,4]{0,1:T(4,128)}, u32[]{:S(2)}) copy-start(f32[512,4]{0,1:T(4,128)} %copy.183) | copy-start | bytes 24580
  237.4 58.9 %copy-start.39 = (f32[4,512]{1,0:T(4,128)S(1)}, f32[4,512]{1,0:T(4,128)}, u32[]{:S(2)}) copy-start(f32[4,512]{1,0:T(4,128)} %get-tuple-element.36) | copy-start | bytes 24580
  237.5 58.9 %copy-start.40 = (f32[4,512]{1,0:T(4,128)S(1)}, f32[4,512]{1,0:T(4,128)}, u32[]{:S(2)}) copy-start(f32[4,512]{1,0:T(4,128)} %get-tuple-element.37) | copy-start | bytes 24580
  237.5 58.9 %copy-start.50 = (f32[512]{0:T(512)S(1)}, f32[512]{0:T(512)}, u32[]{:S(2)}) copy-start(f32[512]{0:T(512)} %copy-done.49) | copy-start | bytes 6148
  237.5 58.9 %copy-start.64 = (pred[512]{0:T(512)(128)(4,1)S(1)}, pred[512]{0:T(512)(128)(4,1)}, u32[]{:S(2)}) copy-start(pred[512]{0:T(512)(128)(4,1)} %copy-done.63) | copy-start | bytes 1540
  237.5 26.4 %collective-permute-start.7 = (bf16[4,128,512]{1,2,0:T(8,128)(2,1)S(1)}, bf16[4,128,512]{1,2,0:T(8,128)(2,1)S(1)}, u32[]{:S(2)}, u32[]{:S(2)}) collective-permute-start(bf16[4,128,512]{1,2,0:T(8,128)(2,1)S(1)} %get-tuple-element.56), channel_id=1, source_target_pairs={{0,4},{1,5},{2,6},{3,7},{4,0},{5,1},{6,2},{7,3},{8,12},{9,13},{10,... | collective-permute-start | bytes 1572872 | tf_op jit(solution)/shard_map/ppermute | solution.py:11
  265.2 13.3 %collective-permute-start.8 = (bf16[4,128,512]{1,2,0:T(8,128)(2,1)S(1)}, bf16[4,128,512]{1,2,0:T(8,128)(2,1)S(1)}, u32[]{:S(2)}, u32[]{:S(2)}) collective-permute-start(bf16[4,128,512]{1,2,0:T(8,128)(2,1)S(1)} %get-tuple-element.57), channel_id=1, source_target_pairs={{0,8},{1,9},{2,10},{3,11},{4,12},{5,13},{6,14},{7,15},{8,0},{9,1},... | collective-permute-start | bytes 1572872 | tf_op jit(solution)/shard_map/ppermute | solution.py:11
  280.6 14.1 %collective-permute-start.9 = (bf16[4,128,512]{1,2,0:T(8,128)(2,1)S(1)}, bf16[4,128,512]{1,2,0:T(8,128)(2,1)S(1)}, u32[]{:S(2)}, u32[]{:S(2)}) collective-permute-start(bf16[4,128,512]{1,2,0:T(8,128)(2,1)S(1)} %get-tuple-element.58), channel_id=1, source_target_pairs={{0,16},{1,17},{2,18},{3,19},{4,20},{5,21},{6,22},{7,23},{8,24},{9,... | collective-permute-start | bytes 1572872 | tf_op jit(solution)/shard_map/ppermute | solution.py:11
  (57 other events, 1259.4 us)
Sparse Core Ops, SparseCore 0:
  9.8 68.7 all-gather.4
  80.4 64.7 all-gather.2
  213.0 137.3 reduce-scatter.8
  353.5 139.3 reduce-scatter.6
  495.9 143.0 reduce-scatter.10
  642.1 143.5 reduce-scatter.4
where the time goes:
time: 798 us; the launch traced here: 793 us
  waiting for transfers between devices  533 us (67%)
  blocking collectives  132 us (17%)
  local copies, waits for them, and re-layouts  42.7 us (5%)
  other arithmetic  33.6 us (4%)
  matrix products  28.4 us (4%)
  between operations  15.4 us (2%)
    reduce_scatter x4, waiting for transfers between devices, shards(): lax.psum_scatter(shortened(partials), 'tensor', scatter_dimension=1, tile...  442 us
    ppermute x10, waiting for transfers between devices, from_partner(): lax.ppermute(value, axis, [(i, i ^ 1 << distance) for i in range(lax.axis...  90.8 us
    all_gather x1, blocking collectives, shards(): lax.all_gather(k_cot, 'tensor', axis=1, tiled=True)  47.8 us
    psum x1, blocking collectives, shards(): lax.psum(angle_local.astype(jnp.bfloat16), 'dp').astype(jnp.float32)  45.4 us
    all_gather x1, blocking collectives, shards(): lax.all_gather(v_cot, 'tensor', axis=1, tiled=True)  39.2 us
    gather x10, local copies, waits for them, and re-layouts, forward_sections(): jnp.take(angles[:, section_num], pair_index(channels, section_bit), axis=1)  19.6 us
    unnamed x141, local copies, waits for them, and re-layouts  19 us
  transfers between devices with their start and end apart: 16, of which 11 were waited for; matrix products, arithmetic and copies ran while one was open for 12% of the time, Pallas kernels for 0%

commit v1 on v0

v1 whole, which is shorter than its diff:
```python
import jax
import jax.numpy as jnp
from jax import lax
from jax.experimental import pallas as pl
from jax.experimental.pallas import tpu as pltpu
from jax.sharding import PartitionSpec as P

F32 = jnp.float32
BF16 = jnp.bfloat16
MESH = pl.DeviceIdType.MESH
N = 32
DP = 8
CH = 512
SUB = 16
TOK = 128
SEC = 5
ROWS = 576
HALF = 288
NT = (((1,), (1,)), ((), ()))


def dot(a, b):
    return jnp.dot(a, b, preferred_element_type=F32)


def dot_nt(a, b):
    return lax.dot_general(a, b, NT, preferred_element_type=F32)


def eye(n):
    r = lax.broadcasted_iota(jnp.int32, (n, n), 0)
    c = lax.broadcasted_iota(jnp.int32, (n, n), 1)
    return jnp.where(r == c, 1.0, 0.0).astype(BF16)


def loop(lo, hi, fn, unroll=1):
    def step(i, carry):
        fn(i)
        return carry

    lax.fori_loop(lo, hi, step, 0, unroll=unroll)


def dequantize(packed, scale, out, width):
    def chunk(i):
        cols = pl.ds(pl.multiple_of(i * 128, 128), 128)
        spread = scale[:, cols].astype(F32)
        for g in range(8):
            rows = slice(16 * g, 16 * g + 16)
            word = packed[rows, cols].astype(jnp.int32)
            s = jnp.broadcast_to(spread[g : g + 1, :], (16, 128))
            for plane in range(4):
                digit = (word >> (4 * plane)) & 15 if plane < 3 else word >> 12
                value = (digit.astype(F32) - 7.5) * s
                out[128 * plane + 16 * g : 128 * plane + 16 * g + 16, cols] = value.astype(BF16)

    loop(0, width // 128, chunk)


def add_rows(dst, base, rows, srcs, out=None, out_base=0):
    def step(i):
        off = pl.multiple_of(i * 96, 96)
        total = dst[base, pl.ds(rows[0] + off, 96), :].astype(F32)
        for ref, index, first in srcs:
            total = total + ref[index + (pl.ds(first + off, 96), slice(None))].astype(F32)
        if out is None:
            dst[base, pl.ds(rows[0] + off, 96), :] = total.astype(BF16)
        else:
            out[out_base, pl.ds(rows[0] + off, 96), :] = total.astype(BF16)

    loop(0, (rows[1] - rows[0]) // 96, step)


def kernel(
    tok, mix, ang, qp, qs, kp, ks, vp, vs, op, os_, qc, kc, vc, oc,
    q_out, k_out, v_out, o_out, tg, mg, ang_out,
    packq, packk, packv, packo, wq, wk, wv, wo, perm,
    tok_t, hin, st, h5s, h5t, hl, ccos, csin,
    ag, part, ra, rx1, rx2, accx, rz, acc, kvt, bks, bkr, gs, gt, angbuf, angd,
    ld, s1, r1, s2, r2, s3, r3, s4, r4, ag_s, ag_r, ag_sib, ra_s, ra_r, rx1_s, rx1_r,
    rx2_s, rx2_r, rz_s, rz_r, sd, rd,
):
    d = lax.axis_index("dp")
    t = lax.axis_index("tensor")
    x = lax.div(t, 8)
    z = lax.rem(lax.div(t, 2), 4)
    c = lax.rem(t, 2)
    xp, xm, x2 = lax.rem(x + 1, 4), lax.rem(x + 3, 4), lax.rem(x + 2, 4)

    def dev(x_, z_, c_):
        return (x_ * 4 + z_) * 2 + c_

    sib = dev(x, z, 1 - c)

    def send(src, dst, ssem, rsem, peer, axis="tensor"):
        return pltpu.make_async_remote_copy(
            src_ref=src, dst_ref=dst, send_sem=ssem, recv_sem=rsem,
            device_id={axis: peer}, device_id_type=MESH,
        )

    loads = [
        pltpu.make_async_copy(src, dst, ld.at[i])
        for i, (src, dst) in enumerate(((kp, packk), (vp, packv), (qp, packq), (op, packo)))
    ]
    for load in loads:
        load.start()
    bar = pltpu.get_barrier_semaphore()
    loop(1, N, lambda i: pl.semaphore_signal(
        bar, inc=1, device_id={"tensor": lax.rem(t + i, N)}, device_id_type=MESH))
    loop(1, DP, lambda i: pl.semaphore_signal(
        bar, inc=1, device_id={"dp": lax.rem(d + i, DP)}, device_id_type=MESH))

    r = lax.broadcasted_iota(jnp.int32, (CH, CH), 0)
    col = lax.broadcasted_iota(jnp.int32, (CH, CH), 1)
    perm[...] = jnp.where(col == 4 * (r & 127) + (r >> 7), 1.0, 0.0).astype(BF16)
    tok_t[0] = dot_nt(perm[...], tok[...]).astype(BF16)
    tok_t[1] = dot_nt(perm[...], mix[...]).astype(BF16)
    own = c * 16 + x * 4 + z
    ag[own, 0:256, :] = dot_nt(eye(256), qc[...]).astype(BF16)
    ag[own, 256:512, :] = dot_nt(eye(256), oc[...]).astype(BF16)
    ag[own, 512:544, :] = dot_nt(eye(32), kc[...]).astype(BF16)
    ag[own, 544:576, :] = dot_nt(eye(32), vc[...]).astype(BF16)
    pl.semaphore_wait(bar, N - 1 + DP - 1)

    def mine(p):
        return pl.ds(pl.multiple_of(p * SUB, SUB), SUB)

    def in_copy(p, slot):
        return send(tok_t.at[:, mine(p), :], hin.at[slot], s1.at[p], r1.at[slot], p)

    loop(1, N, lambda i: in_copy(lax.rem(t + i, N), t).start())
    hin[t] = tok_t[:, mine(t), :]

    def ag_copy(k, x_, z_, peer, sems):
        slot = c * 16 + x_ * 4 + z_
        return send(ag.at[slot], ag.at[slot], ag_s.at[k], sems.at[x_ * 4 + z_], peer)

    def ag_wait(x_, z_, sems):
        slot = c * 16 + x_ * 4 + z_
        send(ag.at[slot], ag.at[slot], ag_s.at[0], sems.at[x_ * 4 + z_], sib).wait_recv()

    def zrel(dz):
        return lax.rem(z + dz, 4)

    for dz in (1, 2, 3):
        ag_copy(dz - 1, x, z, dev(x, zrel(dz), c), ag_r).start()

    def ag_row(dz):
        ag_copy(3 + 2 * dz, x, zrel(dz), dev(xp, z, c), ag_r).start()
        ag_copy(4 + 2 * dz, x, zrel(dz), dev(xm, z, c), ag_r).start()
        ag_copy(15 + dz, x, zrel(dz), sib, ag_sib).start()

    ag_row(0)

    lanes = lax.broadcasted_iota(jnp.int32, (SUB, TOK), 1)
    subs = lax.broadcasted_iota(jnp.int32, (SUB, TOK), 0)
    pick = lanes == 4 * subs + (64 * c + x)
    window = 128 * lax.div(lax.rem(t, 8), 2)

    def factors(pr):
        where = pl.ds(pl.multiple_of(pr * CH + window, 128), 128)
        for j in range(4):
            for n in range(SEC):
                row = jnp.broadcast_to(ang[j, n : n + 1, where], (SUB, TOK))
                angle = jnp.sum(jnp.where(pick, row, 0.0), axis=1, keepdims=True)
                square = angle * angle
                inverse = 1.0 / (1.0 + square)
                ccos[n, pr, j] = jnp.broadcast_to((1.0 - square) * inverse, (SUB, TOK))
                csin[n, pr, j] = jnp.broadcast_to(2.0 * angle * inverse, (SUB, TOK))

    loop(0, 16, factors)
    loads[0].wait()
    dequantize(packk, ks, wk, 1024)
    loads[1].wait()
    dequantize(packv, vs, wv, 1024)

    def wait_in(i):
        p = lax.rem(t + i, N)
        in_copy(p, p).wait_recv()

    loop(1, N, wait_in)

    def pair_of(n, pr):
        sh = 4 - n
        low = ((pr >> sh) << (sh + 1)) + (pr & ((1 << sh) - 1))
        return low, low + (1 << sh)

    def state(n, blk, j):
        if n == 0:
            return hin[blk, 0 if j < 3 else 1].astype(F32)
        return st[n - 1, blk, j].astype(F32)

    for n in range(SEC):

        def forward(pr, n=n):
            t0, t1 = pair_of(n, pr)
            for j in range(4):
                a, b = state(n, t0, j), state(n, t1, j)
                cs, sn = ccos[n, pr, j], csin[n, pr, j]
                low = (cs * a - sn * b).astype(BF16)
                high = (sn * a + cs * b).astype(BF16)
                if n < SEC - 1:
                    st[n, t0, j] = low
                    st[n, t1, j] = high
                else:
                    h5s[t0, j] = low
                    h5s[t1, j] = high

        loop(0, 16, forward)

    def h5_copy(p, src):
        return send(h5s.at[p], h5t.at[:, mine(src), :], s2.at[p], r2.at[src], p)

    loop(1, N, lambda i: h5_copy(lax.rem(t + i, N), t).start())
    h5t[:, mine(t), :] = h5s[t]

    for dz in (1, 2, 3):
        ag_wait(x, zrel(dz), ag_r)
        ag_row(dz)
    loads[2].wait()
    dequantize(packq, qs, wq, 8192)
    for dz in range(4):
        ag_wait(xm, zrel(dz), ag_r)
        if dz % 2 == 0:
            ag_copy(11 + dz // 2, xm, zrel(dz), dev(xp, z, c), ag_r).start()
        ag_copy(19 + dz, xm, zrel(dz), sib, ag_sib).start()
        ag_wait(xp, zrel(dz), ag_r)
        if dz % 2 == 1:
            ag_copy(13 + dz // 2, xp, zrel(dz), dev(xm, z, c), ag_r).start()
        ag_copy(23 + dz, xp, zrel(dz), sib, ag_sib).start()
    loads[3].wait()
    dequantize(packo, os_, wo, 8192)
    for dz in range(4):
        ag_wait(x2, zrel(dz), ag_r)
        ag_copy(27 + dz, x2, zrel(dz), sib, ag_sib).start()

    def wait_h5(i):
        p = lax.rem(t + i, N)
        h5_copy(p, p).wait_recv()

    loop(1, N, wait_h5)
    for j in range(4):
        hl[j] = dot_nt(eye(TOK), h5t[j]).astype(BF16)
    for j, w, first in ((1, wk, 512), (2, wv, 544)):

        def narrow(i, j=j, w=w, first=first):
            cols = pl.ds(pl.multiple_of(i * 128, 128), 128)
            piece = dot(hl[j], w[:, cols]).astype(BF16)
            turned = dot_nt(eye(TOK), piece).astype(BF16)
            for k in range(4):
                z_ = 2 * lax.rem(i, 2) + k // 2
                slot = ((k % 2) * 4 + z_) * 4 + lax.div(i, 2)
                part[slot, first : first + 32, :] = turned[32 * k : 32 * k + 32, :]

        loop(0, 8, narrow)

    def wide(zp):
        def column(x_):
            cols = pl.ds(pl.multiple_of((x_ * 4 + zp) * 512, 512), 512)
            for j, w, first in ((0, wq, 0), (3, wo, 256)):
                piece = dot(hl[j], w[:, cols]).astype(BF16)
                for c_ in range(2):
                    for half in range(2):
                        at = c_ * 256 + half * 128
                        rows = slice(first + half * 128, first + half * 128 + 128)
                        part[(c_ * 4 + zp) * 4 + x_, rows, :] = piece[:, at : at + 128]

        loop(0, 4, column)

    def piece_z(p):
        return lax.rem(z + 1 + p, 4)

    def base(zp):
        return (c * 4 + zp) * 4

    def a_copy(p):
        zp = piece_z(p)
        return send(
            part.at[pl.ds(((1 - c) * 4 + zp) * 4, 4)], ra.at[pl.ds(zp * 4, 4)],
            ra_s.at[p], ra_r.at[p], sib,
        )

    def x1_copy(p, way):
        zp = piece_z(p)
        return send(
            part.at[base(zp) + x2, pl.ds(way * HALF, HALF), :], rx1.at[zp, way],
            rx1_s.at[2 * p + way], rx1_r.at[2 * p + way], dev(xm if way else xp, z, c),
        )

    def x2_copy(p, way):
        zp = piece_z(p)
        to = xm if way else xp
        return send(
            part.at[base(zp) + to], rx2.at[zp, way],
            rx2_s.at[2 * p + way], rx2_r.at[2 * p + way], dev(to, z, c),
        )

    def z_copy(p, src):
        zp = piece_z(p)
        return send(accx.at[zp], rz.at[src], rz_s.at[p], rz_r.at[src], dev(x, zp, c))

    def stage_x1(p):
        zp = piece_z(p)
        a_copy(p).wait_recv()
        add_rows(part, base(zp) + x2, (0, ROWS), [(ra, (zp * 4 + x2,), 0)])
        x1_copy(p, 0).start()
        x1_copy(p, 1).start()
        for x_ in (xp, xm, x):
            add_rows(part, base(zp) + x_, (0, ROWS), [(ra, (zp * 4 + x_,), 0)])

    def stage_x2(p):
        zp = piece_z(p)
        x1_copy(p, 0).wait_recv()
        add_rows(part, base(zp) + xp, (0, HALF), [(rx1, (zp, 0), 0)])
        x2_copy(p, 0).start()
        x1_copy(p, 1).wait_recv()
        add_rows(part, base(zp) + xm, (HALF, ROWS), [(rx1, (zp, 1), 0)])
        x2_copy(p, 1).start()

    def stage_x3(p):
        zp = piece_z(p)
        x2_copy(p, 0).wait_recv()
        x2_copy(p, 1).wait_recv()
        add_rows(part, base(zp) + x, (0, ROWS), [(rx2, (zp, 0), 0), (rx2, (zp, 1), 0)], accx, zp)
        if p < 3:
            z_copy(p, z).start()

    for p in range(4):
        wide(piece_z(p))
        a_copy(p).start()
        if p:
            stage_x1(p - 1)
    stage_x1(3)

    for x_ in range(4):
        for z_ in range(4):
            slot = (1 - c) * 16 + x_ * 4 + z_
            send(
                ag.at[slot], ag.at[slot], ag_s.at[0], ag_sib.at[x_ * 4 + z_], sib
            ).wait_recv()

    def back_wide(j, w, first):
        acc[...] = jnp.zeros_like(acc)

        def step(i):
            rhs = jnp.concatenate(
                [ag[i, first : first + 256, :], ag[16 + i, first : first + 256, :]], axis=0
            )
            acc[...] += dot(w[:, pl.ds(pl.multiple_of(i * 512, 512), 512)], rhs)

        loop(0, 16, step)
        bks[j] = acc[...].astype(BF16)

    def back_narrow(j, w, first):
        def turn(i):
            for c_ in range(2):
                kvt[pl.ds(pl.multiple_of(i * 64 + c_ * 32, 32), 32), :] = ag[
                    c_ * 16 + i, first : first + 32, :
                ]

        loop(0, 16, turn)
        bks[j] = dot(w[...], kvt[...]).astype(BF16)

    back_wide(0, wq, 0)
    stage_x2(0)
    back_narrow(1, wk, 512)
    back_narrow(2, wv, 544)
    stage_x2(1)
    back_wide(3, wo, 256)
    stage_x2(2)

    def back_copy(p, slot):
        return send(bks.at[:, mine(p), :], bkr.at[slot], s3.at[p], r3.at[slot], p)

    loop(1, N, lambda i: back_copy(lax.rem(t + i, N), t).start())
    bkr[t] = bks[:, mine(t), :]
    stage_x2(3)
    for p in range(4):
        stage_x3(p)

    def wait_back(i):
        p = lax.rem(t + i, N)
        back_copy(p, p).wait_recv()

    loop(1, N, wait_back)
    jn = lanes & 31

    for n in reversed(range(SEC)):

        def backward(pr, n=n):
            t0, t1 = pair_of(n, pr)
            grads = jnp.zeros((SUB, TOK), F32)
            lows, highs = [], []
            for j in range(4):
                cs, sn = ccos[n, pr, j], csin[n, pr, j]
                gl, gu = bkr[t0, j].astype(F32), bkr[t1, j].astype(F32)
                low = cs * gl + sn * gu
                high = cs * gu - sn * gl
                e = state(n, t0, j) * high - state(n, t1, j) * low
                total = jnp.sum(e, axis=1, keepdims=True) * (1.0 + cs)
                grads = jnp.where(jn == j * SEC + n, total, grads)
                lows.append(low)
                highs.append(high)
                if n:
                    bkr[t0, j] = low.astype(BF16)
                    bkr[t1, j] = high.astype(BF16)
            if n == 0:
                for blk, parts in ((t0, lows), (t1, highs)):
                    gs[blk, 0] = (parts[0] + parts[1] + parts[2]).astype(BF16)
                    gs[blk, 1] = parts[3].astype(BF16)
            for blk in (t0, t1):
                whole = grads if n == SEC - 1 else angbuf[blk] + grads
                if n:
                    angbuf[blk] = whole
                else:
                    top = whole.astype(BF16).astype(F32)
                    gs[blk, 2] = jnp.where(lanes < 32, top, whole - top).astype(BF16)

        loop(0, 16, backward)

    def out_copy(p, src):
        return send(gs.at[p], gt.at[:, mine(src), :], s4.at[p], r4.at[src], p)

    loop(1, N, lambda i: out_copy(lax.rem(t + i, N), t).start())
    gt[:, mine(t), :] = gs[t]

    for p in range(3):
        src = lax.rem(z + 1 + p, 4)
        z_copy(0, src).wait_recv()
    total = accx[z].astype(F32)
    for p in range(3):
        total = total + rz[lax.rem(z + 1 + p, 4)].astype(F32)
    total = total.astype(BF16)
    q_out[:, 0:128] = total[0:128]
    q_out[:, 128:256] = total[128:256]
    o_out[:, 0:128] = total[256:384]
    o_out[:, 128:256] = total[384:512]
    k_out[...] = dot_nt(eye(TOK), total[512:544]).astype(BF16)
    v_out[...] = dot_nt(eye(TOK), total[544:576]).astype(BF16)

    def wait_out(i):
        p = lax.rem(t + i, N)
        out_copy(p, p).wait_recv()

    loop(1, N, wait_out)

    def natural(k):
        turned = dot_nt(eye(TOK), gt[k]).astype(BF16)
        return dot(turned, perm[...])

    both = natural(2)
    angd[d] = both[0:32] + both[32:64]

    def ang_copy(p, slot):
        return send(angd.at[slot], angd.at[slot], sd.at[p], rd.at[slot], p, "dp")

    loop(1, DP, lambda i: ang_copy(lax.rem(d + i, DP), d).start())
    tg[...] = natural(0).astype(BF16)
    mg[...] = natural(1).astype(BF16)

    def wait_ang(i):
        p = lax.rem(d + i, DP)
        ang_copy(p, p).wait_recv()

    loop(1, DP, wait_ang)
    grads = angd[0]
    for i in range(1, DP):
        grads = grads + angd[i]
    for j in range(4):
        ang_out[j] = grads[j * SEC : j * SEC + SEC]

    def drain(i):
        p = lax.rem(t + i, N)
        in_copy(p, t).wait_send()
        h5_copy(p, t).wait_send()
        back_copy(p, t).wait_send()
        out_copy(p, t).wait_send()

    loop(1, N, drain)
    loop(0, 31, lambda i: ag_copy(i, x, z, sib, ag_r).wait_send())
    for p in range(4):
        a_copy(p).wait_send()
        for way in range(2):
            x1_copy(p, way).wait_send()
            x2_copy(p, way).wait_send()
        if p < 3:
            z_copy(p, z).wait_send()
    loop(1, DP, lambda i: ang_copy(lax.rem(d + i, DP), d).wait_send())


def shards(*args):
    def vm(shape, dtype=BF16):
        return pltpu.VMEM(shape, dtype)

    def sem(n):
        return pltpu.SemaphoreType.DMA((n,))

    scratch = [
        vm((128, 8192), F32), vm((128, 1024), F32), vm((128, 1024), F32), vm((128, 8192), F32),
        vm((CH, 8192)), vm((CH, 1024)), vm((CH, 1024)), vm((CH, 8192)),
        vm((CH, CH)),
        vm((2, CH, TOK)), vm((N, 2, SUB, TOK)),
        vm((SEC - 1, N, 4, SUB, TOK)), vm((N, 4, SUB, TOK)),
        vm((4, CH, TOK)), vm((4, TOK, CH)),
        vm((SEC, 16, 4, SUB, TOK), F32), vm((SEC, 16, 4, SUB, TOK), F32),
        vm((N, ROWS, TOK)), vm((N, ROWS, TOK)),
        vm((16, ROWS, TOK)),
        vm((4, 2, HALF, TOK)), vm((4, 2, ROWS, TOK)),
        vm((4, ROWS, TOK)), vm((4, ROWS, TOK)),
        vm((CH, TOK), F32), vm((1024, TOK)),
        vm((4, CH, TOK)), vm((N, 4, SUB, TOK)),
        vm((N, 3, SUB, TOK)), vm((3, CH, TOK)),
        vm((N, SUB, TOK), F32), vm((DP, 32, CH), F32),
        sem(4), sem(N), sem(N), sem(N), sem(N), sem(N), sem(N), sem(N), sem(N),
        sem(31), sem(16), sem(16), sem(4), sem(4), sem(8), sem(8), sem(8), sem(8),
        sem(4), sem(4), sem(DP), sem(DP),
    ]
    outs = [
        jax.ShapeDtypeStruct((TOK, 256), BF16),
        jax.ShapeDtypeStruct((TOK, 32), BF16),
        jax.ShapeDtypeStruct((TOK, 32), BF16),
        jax.ShapeDtypeStruct((TOK, 256), BF16),
        jax.ShapeDtypeStruct((TOK, CH), BF16),
        jax.ShapeDtypeStruct((TOK, CH), BF16),
        jax.ShapeDtypeStruct((4, SEC, CH), F32),
    ]
    in_vmem = pl.BlockSpec(memory_space=pltpu.VMEM)
    in_any = pl.BlockSpec(memory_space=pl.ANY)
    return pl.pallas_call(
        kernel,
        out_shape=outs,
        in_specs=[in_any if i in (3, 5, 7, 9) else in_vmem for i in range(15)],
        out_specs=[in_vmem] * 7,
        scratch_shapes=scratch,
        compiler_params=pltpu.CompilerParams(
            collective_id=0, has_side_effects=True, vmem_limit_bytes=62 * 1024 * 1024
        ),
        cost_estimate=pl.CostEstimate(
            flops=4 * TOK * CH * 18432, bytes_accessed=12_000_000, transcendentals=0
        ),
    )(*args)


def solution(mesh):
    both = P("dp", "tensor")
    rows = P("tensor", None)
    return jax.shard_map(
        shards,
        mesh=mesh,
        in_specs=(both, both, P(), rows, rows, rows, rows, rows, rows, rows, rows)
        + (both, both, both, both),
        out_specs=(both, both, both, both, both, both, P(None, None, "tensor")),
        check_vma=False,
    )
```

time: 798 us -> 152 us (0.19)
  waiting for transfers between devices: 533 us -> 0 us
  Pallas kernels: 0 us -> 134 us
  blocking collectives: 132 us -> 0 us
  other arithmetic: 33.6 us -> 0 us
  matrix products: 28.4 us -> 0 us
  local copies, waits for them, and re-layouts: 42.7 us -> 15.7 us
  between operations: 15.4 us -> 0.64 us
    reduce_scatter x4 -> x0, waiting for transfers between devices: 442 us -> none  [shards(): lax.psum_scatter(shortened(partials), 'tensor', scatter_dimension=1, tile...]
    pallas_call x0 -> x1, Pallas kernels: none -> 134 us  [shards(): pl.pallas_call(kernel, out_shape=outs, in_specs=[in_any if i in (3, 5, 7,...]
    ppermute x10 -> x0, waiting for transfers between devices: 90.8 us -> none  [from_partner(): lax.ppermute(value, axis, [(i, i ^ 1 << distance) for i in range(lax.axis...]
    all_gather x2 -> x0, blocking collectives: 87 us -> none  [the longest x1 47.8 us: shards(): lax.all_gather(k_cot, 'tensor', axis=1, tiled=True)]
    psum x1 -> x0, blocking collectives: 45.4 us -> none  [shards(): lax.psum(angle_local.astype(jnp.bfloat16), 'dp').astype(jnp.float32)]
    dot_general x8 -> x0, matrix products: 28.4 us -> none  [the longest x4 15.3 us: project_rows(): lax.dot_general(split_rows, planes, (((0, 2), (0, 1)), ((), ())), preferr...]
    gather x10 -> x0, local copies, waits for them, and re-layouts: 19.6 us -> none  [forward_sections(): jnp.take(angles[:, section_num], pair_index(channels, section_bit), axis=1)]
    convert_element_type x9 -> x0, other arithmetic: 16.9 us -> none  [the longest x2 12.9 us: dequantize(): ((digit - 7.5) * spread).reshape(word_rows, columns).astype(jnp.bfloat16)]
  transfers between devices with their start and end apart: 16 -> 0, of which waited for: 11 -> 0; matrix products, arithmetic and copies ran while one was open for 12% -> 0% of each run, Pallas kernels for 0% -> 0%
where the time goes in v1:
time: 152 us; the launch traced here: 150 us
  Pallas kernels  134 us (88%)
  local copies, waits for them, and re-layouts  15.7 us (10%)
    pallas_call x1, Pallas kernels, shards(): pl.pallas_call(kernel, out_shape=outs, in_specs=[in_any if i in (3, 5, 7,...  134 us
    unnamed x7, local copies, waits for them, and re-layouts  11.4 us
    pallas_call x3, local copies, waits for them, and re-layouts, shards(): pl.pallas_call(kernel, out_shape=outs, in_specs=[in_any if i in (3, 5, 7,...  4.35 us

profile of v1, /device:TPU:1, one launch (start us, length us, event | category | flops | bytes accessed | tf_op | source)
XLA Modules:
  0.0 150.4 jit_solution(13914636573805709062)
XLA Ops:
  0.6 1.4 copy.23.kc
  2.0 1.4 copy.24.vc
  3.5 2.5 %copy.22.ang = f32[4,5,8192]{2,1,0:T(8,128)} copy(f32[4,5,8192]{2,0,1:T(4,128)} %param.17) | data formatting | bytes 1310720 | tf_op args[2]
  5.9 134.0 %shard_map.198 = (bf16[128,256]{1,0:T(8,128)(2,1)}, bf16[128,32]{1,0:T(8,128)(2,1)}, bf16[128,32]{1,0:T(8,128)(2,1)}, bf16[128,256]{1,0:T(8,128)(2,1)}, bf16[128...) custom-call(bf16[128,512]{1,0:T(8,128)(2,1)} %tok.1, bf16[128,512]{1,0:T(8,128)(2,1)} %mix.1, ...), custom_call_target="tpu_custom_call" | custom-call | flops 4831838208 | bytes 12000000 | tf_op jit(solution)/shard_map/pallas_call | solution.py:529
  139.9 1.4 copy.25
  141.4 1.4 copy.26
  142.8 1.5 copy.27
  144.3 1.5 copy.32
  145.7 1.5 copy.33
  147.2 1.6 %copy.34 = bf16[128,512]{1,0:T(8,128)(2,1)} copy(bf16[128,512]{1,0:T(8,128)(2,1)} %get-tuple-element.25) | data formatting | bytes 262144
  148.8 1.6 %copy.35 = bf16[128,512]{1,0:T(8,128)(2,1)} copy(bf16[128,512]{1,0:T(8,128)(2,1)} %get-tuple-element.26) | data formatting | bytes 262144

commit v2 on v1

--- a/solution.py
+++ b/solution.py
@@ -9,7 +9,7 @@
 BF16 = jnp.bfloat16
 MESH = pl.DeviceIdType.MESH
 N = 32
-DP = 8
+BU = 2
 CH = 512
 SUB = 16
 TOK = 128
@@ -41,9 +41,9 @@
     lax.fori_loop(lo, hi, step, 0, unroll=unroll)
 
 
-def dequantize(packed, scale, out, width):
+def dequantize(packed, scale, out, first, width):
     def chunk(i):
-        cols = pl.ds(pl.multiple_of(i * 128, 128), 128)
+        cols = pl.ds(pl.multiple_of(first + i * 128, 128), 128)
         spread = scale[:, cols].astype(F32)
         for g in range(8):
             rows = slice(16 * g, 16 * g + 16)
@@ -76,9 +76,9 @@
     q_out, k_out, v_out, o_out, tg, mg, ang_out,
     packq, packk, packv, packo, wq, wk, wv, wo, perm,
     tok_t, hin, st, h5s, h5t, hl, ccos, csin,
-    ag, part, ra, rx1, rx2, accx, rz, acc, kvt, bks, bkr, gs, gt, angbuf, angd,
+    ag, part, ra, rx1, rx2, accx, rz, acc, bks, bkr, gb, gs, gt, angy, angz, spread, angs, angt,
     ld, s1, r1, s2, r2, s3, r3, s4, r4, ag_s, ag_r, ag_sib, ra_s, ra_r, rx1_s, rx1_r,
-    rx2_s, rx2_r, rz_s, rz_r, sd, rd,
+    rx2_s, rx2_r, rz_s, rz_r, sd, rd, s5, r5,
 ):
     d = lax.axis_index("dp")
     t = lax.axis_index("tensor")
@@ -91,6 +91,9 @@
         return (x_ * 4 + z_) * 2 + c_
 
     sib = dev(x, z, 1 - c)
+    y, zh = lax.div(d, 2), lax.rem(d, 2)
+    far = y * 2 + 1 - zh
+    dp_peers = [lax.rem(y + i, 4) * 2 + zh for i in (1, 2, 3)] + [far]
 
     def send(src, dst, ssem, rsem, peer, axis="tensor"):
         return pltpu.make_async_remote_copy(
@@ -107,8 +110,8 @@
     bar = pltpu.get_barrier_semaphore()
     loop(1, N, lambda i: pl.semaphore_signal(
         bar, inc=1, device_id={"tensor": lax.rem(t + i, N)}, device_id_type=MESH))
-    loop(1, DP, lambda i: pl.semaphore_signal(
-        bar, inc=1, device_id={"dp": lax.rem(d + i, DP)}, device_id_type=MESH))
+    for peer in dp_peers:
+        pl.semaphore_signal(bar, inc=1, device_id={"dp": peer}, device_id_type=MESH)
 
     r = lax.broadcasted_iota(jnp.int32, (CH, CH), 0)
     col = lax.broadcasted_iota(jnp.int32, (CH, CH), 1)
@@ -118,9 +121,9 @@
     own = c * 16 + x * 4 + z
     ag[own, 0:256, :] = dot_nt(eye(256), qc[...]).astype(BF16)
     ag[own, 256:512, :] = dot_nt(eye(256), oc[...]).astype(BF16)
-    ag[own, 512:544, :] = dot_nt(eye(32), kc[...]).astype(BF16)
-    ag[own, 544:576, :] = dot_nt(eye(32), vc[...]).astype(BF16)
-    pl.semaphore_wait(bar, N - 1 + DP - 1)
+    ag[own, 512:544, :] = kc[...]
+    ag[own, 544:576, :] = vc[...]
+    pl.semaphore_wait(bar, N - 1 + 4)
 
     def mine(p):
         return pl.ds(pl.multiple_of(p * SUB, SUB), SUB)
@@ -161,7 +164,7 @@
         where = pl.ds(pl.multiple_of(pr * CH + window, 128), 128)
         for j in range(4):
             for n in range(SEC):
-                row = jnp.broadcast_to(ang[j, n : n + 1, where], (SUB, TOK))
+                row = jnp.broadcast_to(ang[n, j : j + 1, where], (SUB, TOK))
                 angle = jnp.sum(jnp.where(pick, row, 0.0), axis=1, keepdims=True)
                 square = angle * angle
                 inverse = 1.0 / (1.0 + square)
@@ -170,9 +173,9 @@
 
     loop(0, 16, factors)
     loads[0].wait()
-    dequantize(packk, ks, wk, 1024)
+    dequantize(packk, ks, wk, 0, 1024)
     loads[1].wait()
-    dequantize(packv, vs, wv, 1024)
+    dequantize(packv, vs, wv, 0, 1024)
 
     def wait_in(i):
         p = lax.rem(t + i, N)
@@ -214,12 +217,12 @@
     loop(1, N, lambda i: h5_copy(lax.rem(t + i, N), t).start())
     h5t[:, mine(t), :] = h5s[t]
 
-    for dz in (1, 2, 3):
+    for dz in (1, 3, 2):
         ag_wait(x, zrel(dz), ag_r)
         ag_row(dz)
     loads[2].wait()
-    dequantize(packq, qs, wq, 8192)
     for dz in range(4):
+        dequantize(packq, qs, wq, 2048 * dz, 2048)
         ag_wait(xm, zrel(dz), ag_r)
         if dz % 2 == 0:
             ag_copy(11 + dz // 2, xm, zrel(dz), dev(xp, z, c), ag_r).start()
@@ -229,8 +232,8 @@
             ag_copy(13 + dz // 2, xp, zrel(dz), dev(xm, z, c), ag_r).start()
         ag_copy(23 + dz, xp, zrel(dz), sib, ag_sib).start()
     loads[3].wait()
-    dequantize(packo, os_, wo, 8192)
     for dz in range(4):
+        dequantize(packo, os_, wo, 2048 * dz, 2048)
         ag_wait(x2, zrel(dz), ag_r)
         ag_copy(27 + dz, x2, zrel(dz), sib, ag_sib).start()
 
@@ -238,21 +241,13 @@
         p = lax.rem(t + i, N)
         h5_copy(p, p).wait_recv()
 
-    loop(1, N, wait_h5)
-    for j in range(4):
-        hl[j] = dot_nt(eye(TOK), h5t[j]).astype(BF16)
-    for j, w, first in ((1, wk, 512), (2, wv, 544)):
-
-        def narrow(i, j=j, w=w, first=first):
-            cols = pl.ds(pl.multiple_of(i * 128, 128), 128)
-            piece = dot(hl[j], w[:, cols]).astype(BF16)
-            turned = dot_nt(eye(TOK), piece).astype(BF16)
+    def narrow(j, w, first):
+        piece = dot(hl[j], w[...]).astype(BF16)
+        for i in range(8):
+            turned = dot_nt(eye(TOK), piece[:, 128 * i : 128 * i + 128]).astype(BF16)
             for k in range(4):
-                z_ = 2 * lax.rem(i, 2) + k // 2
-                slot = ((k % 2) * 4 + z_) * 4 + lax.div(i, 2)
+                slot = ((k % 2) * 4 + 2 * (i % 2) + k // 2) * 4 + i // 2
                 part[slot, first : first + 32, :] = turned[32 * k : 32 * k + 32, :]
-
-        loop(0, 8, narrow)
 
     def wide(zp):
         def column(x_):
@@ -325,104 +320,130 @@
         if p < 3:
             z_copy(p, z).start()
 
+    for x_ in range(4):
+        for z_ in range(4):
+            slot = (1 - c) * 16 + x_ * 4 + z_
+            send(
+                ag.at[slot], ag.at[slot], ag_s.at[0], ag_sib.at[x_ * 4 + z_], sib
+            ).wait_recv()
+
+    def back_wide(j, w, first):
+        total = None
+        for quarter in range(4):
+            rhs = jnp.concatenate(
+                [
+                    ag[c_ * 16 + 4 * quarter + i, first : first + 256, :]
+                    for i in range(4)
+                    for c_ in range(2)
+                ],
+                axis=0,
+            )
+            piece = dot(w[:, 2048 * quarter : 2048 * quarter + 2048], rhs)
+            if quarter == 0:
+                acc[...] = piece
+            elif quarter < 3:
+                acc[...] += piece
+            else:
+                bks[j] = (acc[...] + piece).astype(BF16)
+
+    def back_narrow(j, w, first):
+        rhs = jnp.concatenate(
+            [ag[c_ * 16 + i, first : first + 32, :] for i in range(16) for c_ in range(2)], axis=0
+        )
+        bks[j] = dot(w[...], rhs).astype(BF16)
+
+    def back_copy(k, p, slot):
+        js = pl.ds(0, 3) if k == 0 else pl.ds(3, 1)
+        return send(
+            bks.at[js, mine(p), :], bkr.at[slot, js], s3.at[k * N + p], r3.at[k * N + slot], p
+        )
+
+    back_wide(0, wq, 0)
+    back_narrow(1, wk, 512)
+    back_narrow(2, wv, 544)
+    loop(1, N, lambda i: back_copy(0, lax.rem(t + i, N), t).start())
+    back_wide(3, wo, 256)
+    loop(1, N, lambda i: back_copy(1, lax.rem(t + i, N), t).start())
+    bkr[t] = bks[:, mine(t), :]
+
+    loop(1, N, wait_h5)
+    for j in range(4):
+        hl[j] = dot_nt(eye(TOK), h5t[j]).astype(BF16)
+    narrow(1, wk, 512)
+    narrow(2, wv, 544)
     for p in range(4):
         wide(piece_z(p))
         a_copy(p).start()
         if p:
             stage_x1(p - 1)
     stage_x1(3)
-
-    for x_ in range(4):
-        for z_ in range(4):
-            slot = (1 - c) * 16 + x_ * 4 + z_
-            send(
-                ag.at[slot], ag.at[slot], ag_s.at[0], ag_sib.at[x_ * 4 + z_], sib
-            ).wait_recv()
-
-    def back_wide(j, w, first):
-        acc[...] = jnp.zeros_like(acc)
-
-        def step(i):
-            rhs = jnp.concatenate(
-                [ag[i, first : first + 256, :], ag[16 + i, first : first + 256, :]], axis=0
-            )
-            acc[...] += dot(w[:, pl.ds(pl.multiple_of(i * 512, 512), 512)], rhs)
-
-        loop(0, 16, step)
-        bks[j] = acc[...].astype(BF16)
-
-    def back_narrow(j, w, first):
-        def turn(i):
-            for c_ in range(2):
-                kvt[pl.ds(pl.multiple_of(i * 64 + c_ * 32, 32), 32), :] = ag[
-                    c_ * 16 + i, first : first + 32, :
-                ]
-
-        loop(0, 16, turn)
-        bks[j] = dot(w[...], kvt[...]).astype(BF16)
-
-    back_wide(0, wq, 0)
     stage_x2(0)
-    back_narrow(1, wk, 512)
-    back_narrow(2, wv, 544)
     stage_x2(1)
-    back_wide(3, wo, 256)
-    stage_x2(2)
-
-    def back_copy(p, slot):
-        return send(bks.at[:, mine(p), :], bkr.at[slot], s3.at[p], r3.at[slot], p)
-
-    loop(1, N, lambda i: back_copy(lax.rem(t + i, N), t).start())
-    bkr[t] = bks[:, mine(t), :]
-    stage_x2(3)
-    for p in range(4):
-        stage_x3(p)
+    stage_x3(0)
 
     def wait_back(i):
         p = lax.rem(t + i, N)
-        back_copy(p, p).wait_recv()
+        back_copy(0, p, p).wait_recv()
+        back_copy(1, p, p).wait_recv()
 
     loop(1, N, wait_back)
-    jn = lanes & 31
 
     for n in reversed(range(SEC)):
-
-        def backward(pr, n=n):
+        take, put = (bkr, gb) if n % 2 == 0 else (gb, bkr)
+
+        def backward(pr, grads, n=n, take=take, put=put):
             t0, t1 = pair_of(n, pr)
-            grads = jnp.zeros((SUB, TOK), F32)
             lows, highs = [], []
             for j in range(4):
                 cs, sn = ccos[n, pr, j], csin[n, pr, j]
-                gl, gu = bkr[t0, j].astype(F32), bkr[t1, j].astype(F32)
+                gl, gu = take[t0, j].astype(F32), take[t1, j].astype(F32)
                 low = cs * gl + sn * gu
                 high = cs * gu - sn * gl
                 e = state(n, t0, j) * high - state(n, t1, j) * low
                 total = jnp.sum(e, axis=1, keepdims=True) * (1.0 + cs)
-                grads = jnp.where(jn == j * SEC + n, total, grads)
+                grads = jnp.where(lanes == pr * 4 + j, total, grads)
                 lows.append(low)
                 highs.append(high)
                 if n:
-                    bkr[t0, j] = low.astype(BF16)
-                    bkr[t1, j] = high.astype(BF16)
+                    put[t0, j] = low.astype(BF16)
+                    put[t1, j] = high.astype(BF16)
             if n == 0:
                 for blk, parts in ((t0, lows), (t1, highs)):
                     gs[blk, 0] = (parts[0] + parts[1] + parts[2]).astype(BF16)
                     gs[blk, 1] = parts[3].astype(BF16)
-            for blk in (t0, t1):
-                whole = grads if n == SEC - 1 else angbuf[blk] + grads
-                if n:
-                    angbuf[blk] = whole
-                else:
-                    top = whole.astype(BF16).astype(F32)
-                    gs[blk, 2] = jnp.where(lanes < 32, top, whole - top).astype(BF16)
-
-        loop(0, 16, backward)
+            return grads
+
+        angy[y, n] = lax.fori_loop(0, 16, backward, jnp.zeros((SUB, TOK), F32), unroll=BU)
+        if n == 4:
+            stage_x2(2)
+        elif n == 3:
+            stage_x3(1)
+        elif n == 2:
+            stage_x2(3)
+        elif n == 1:
+            stage_x3(2)
+
+    def y_copy(k, slot):
+        return send(angy.at[slot], angy.at[slot], sd.at[k], rd.at[slot], dp_peers[k], "dp")
+
+    for k in range(3):
+        y_copy(k, y).start()
 
     def out_copy(p, src):
         return send(gs.at[p], gt.at[:, mine(src), :], s4.at[p], r4.at[src], p)
 
     loop(1, N, lambda i: out_copy(lax.rem(t + i, N), t).start())
     gt[:, mine(t), :] = gs[t]
+    stage_x3(3)
+    for k in range(3):
+        y_copy(k, lax.rem(y + 1 + k, 4)).wait_recv()
+    for n in range(SEC):
+        angz[zh, n] = ((angy[0, n] + angy[1, n]) + angy[2, n]) + angy[3, n]
+
+    def far_copy(slot):
+        return send(angz.at[slot], angz.at[slot], sd.at[3], rd.at[4], far, "dp")
+
+    far_copy(zh).start()
 
     for p in range(3):
         src = lax.rem(z + 1 + p, 4)
@@ -435,8 +456,32 @@
     q_out[:, 128:256] = total[128:256]
     o_out[:, 0:128] = total[256:384]
     o_out[:, 128:256] = total[384:512]
-    k_out[...] = dot_nt(eye(TOK), total[512:544]).astype(BF16)
-    v_out[...] = dot_nt(eye(TOK), total[544:576]).astype(BF16)
+    k_out[...] = total[512:544]
+    v_out[...] = total[544:576]
+
+    far_copy(1 - zh).wait_recv()
+    for n in range(SEC):
+        whole = angz[0, n] + angz[1, n]
+        for pr in range(16):
+            moved = pltpu.roll(whole, (4 * n - 4 * pr) % TOK, 1)
+            keep = (lanes >= 4 * n) & (lanes < 4 * n + 4)
+            spread[n, pr] = jnp.where(keep, moved, 0.0)
+
+    def message(blk):
+        whole = jnp.zeros((SUB, TOK), F32)
+        for n in range(SEC):
+            sh = 4 - n
+            whole = whole + spread[n, ((blk >> (sh + 1)) << sh) + (blk & ((1 << sh) - 1))]
+        top = whole.astype(BF16).astype(F32)
+        rest = pltpu.roll(whole - top, 32, 1)
+        angs[blk] = jnp.where(lanes < 32, top, rest).astype(BF16)
+
+    def ang_copy(p, src):
+        return send(angs.at[p], angt.at[mine(src), :], s5.at[p], r5.at[src], p)
+
+    loop(0, N, message, unroll=4)
+    loop(1, N, lambda i: ang_copy(lax.rem(t + i, N), t).start())
+    angt[mine(t), :] = angs[t]
 
     def wait_out(i):
         p = lax.rem(t + i, N)
@@ -444,36 +489,27 @@
 
     loop(1, N, wait_out)
 
-    def natural(k):
-        turned = dot_nt(eye(TOK), gt[k]).astype(BF16)
-        return dot(turned, perm[...])
-
-    both = natural(2)
-    angd[d] = both[0:32] + both[32:64]
-
-    def ang_copy(p, slot):
-        return send(angd.at[slot], angd.at[slot], sd.at[p], rd.at[slot], p, "dp")
-
-    loop(1, DP, lambda i: ang_copy(lax.rem(d + i, DP), d).start())
-    tg[...] = natural(0).astype(BF16)
-    mg[...] = natural(1).astype(BF16)
+    def natural(value):
+        return dot(dot_nt(eye(TOK), value).astype(BF16), perm[...])
+
+    tg[...] = natural(gt[0]).astype(BF16)
+    mg[...] = natural(gt[1]).astype(BF16)
 
     def wait_ang(i):
-        p = lax.rem(d + i, DP)
+        p = lax.rem(t + i, N)
         ang_copy(p, p).wait_recv()
 
-    loop(1, DP, wait_ang)
-    grads = angd[0]
-    for i in range(1, DP):
-        grads = grads + angd[i]
-    for j in range(4):
-        ang_out[j] = grads[j * SEC : j * SEC + SEC]
+    loop(1, N, wait_ang)
+    both = natural(angt[...])
+    ang_out[...] = both[0:32] + both[32:64]
 
     def drain(i):
         p = lax.rem(t + i, N)
         in_copy(p, t).wait_send()
         h5_copy(p, t).wait_send()
-        back_copy(p, t).wait_send()
+        back_copy(0, p, t).wait_send()
+        back_copy(1, p, t).wait_send()
+        ang_copy(p, t).wait_send()
         out_copy(p, t).wait_send()
 
     loop(1, N, drain)
@@ -485,7 +521,9 @@
             x2_copy(p, way).wait_send()
         if p < 3:
             z_copy(p, z).wait_send()
-    loop(1, DP, lambda i: ang_copy(lax.rem(d + i, DP), d).wait_send())
+    for k in range(3):
+        y_copy(k, y).wait_send()
+    far_copy(zh).wait_send()
 
 
 def shards(*args):
@@ -507,28 +545,25 @@
         vm((16, ROWS, TOK)),
         vm((4, 2, HALF, TOK)), vm((4, 2, ROWS, TOK)),
         vm((4, ROWS, TOK)), vm((4, ROWS, TOK)),
-        vm((CH, TOK), F32), vm((1024, TOK)),
-        vm((4, CH, TOK)), vm((N, 4, SUB, TOK)),
-        vm((N, 3, SUB, TOK)), vm((3, CH, TOK)),
-        vm((N, SUB, TOK), F32), vm((DP, 32, CH), F32),
-        sem(4), sem(N), sem(N), sem(N), sem(N), sem(N), sem(N), sem(N), sem(N),
+        vm((CH, TOK), F32),
+        vm((4, CH, TOK)), vm((N, 4, SUB, TOK)), vm((N, 4, SUB, TOK)),
+        vm((N, 2, SUB, TOK)), vm((2, CH, TOK)),
+        vm((4, SEC, SUB, TOK), F32), vm((2, SEC, SUB, TOK), F32),
+        vm((SEC, 16, SUB, TOK), F32), vm((N, SUB, TOK)), vm((CH, TOK)),
+        sem(4), sem(N), sem(N), sem(N), sem(N), sem(2 * N), sem(2 * N), sem(N), sem(N),
         sem(31), sem(16), sem(16), sem(4), sem(4), sem(8), sem(8), sem(8), sem(8),
-        sem(4), sem(4), sem(DP), sem(DP),
+        sem(4), sem(4), sem(4), sem(5), sem(N), sem(N),
     ]
-    outs = [
-        jax.ShapeDtypeStruct((TOK, 256), BF16),
-        jax.ShapeDtypeStruct((TOK, 32), BF16),
-        jax.ShapeDtypeStruct((TOK, 32), BF16),
-        jax.ShapeDtypeStruct((TOK, 256), BF16),
-        jax.ShapeDtypeStruct((TOK, CH), BF16),
-        jax.ShapeDtypeStruct((TOK, CH), BF16),
-        jax.ShapeDtypeStruct((4, SEC, CH), F32),
-    ]
+    shapes = [(TOK, 256), (32, TOK), (32, TOK), (TOK, 256), (TOK, CH), (TOK, CH)]
+    outs = [jax.ShapeDtypeStruct(shape, BF16) for shape in shapes]
     in_vmem = pl.BlockSpec(memory_space=pltpu.VMEM)
     in_any = pl.BlockSpec(memory_space=pl.ANY)
-    return pl.pallas_call(
+    args = list(args)
+    args[2] = args[2].transpose(1, 0, 2)
+    args[12], args[13] = args[12].T, args[13].T
+    results = pl.pallas_call(
         kernel,
-        out_shape=outs,
+        out_shape=outs + [jax.ShapeDtypeStruct((32, CH), F32)],
         in_specs=[in_any if i in (3, 5, 7, 9) else in_vmem for i in range(15)],
         out_specs=[in_vmem] * 7,
         scratch_shapes=scratch,
@@ -539,6 +574,21 @@
             flops=4 * TOK * CH * 18432, bytes_accessed=12_000_000, transcendentals=0
         ),
     )(*args)
+
+    def hand_over(*refs):
+        for src, dst in zip(refs[:6], refs[7:13]):
+            dst[...] = src[...]
+        for n in range(SEC):
+            refs[13][n] = refs[6][4 * n : 4 * n + 4, :]
+
+    final = pl.pallas_call(
+        hand_over,
+        out_shape=outs + [jax.ShapeDtypeStruct((SEC, 4, CH), F32)],
+        in_specs=[in_vmem] * 7,
+        out_specs=[in_vmem] * 7,
+    )(*results)
+    q_out, k_out, v_out, o_out, tg, mg, ang = final
+    return q_out, k_out.T, v_out.T, o_out, tg, mg, ang.transpose(1, 0, 2)
 
 
 def solution(mesh):

time: 152 us -> 119 us (0.78)
  Pallas kernels: 134 us -> 118 us
  local copies, waits for them, and re-layouts: 15.7 us -> 0 us
    pallas_call x1 -> x2, Pallas kernels: 134 us -> 118 us  [the longest x1 116 us: shards(): pl.pallas_call(kernel, out_shape=outs + [jax.ShapeDtypeStruct((32, CH), F...]
    unnamed x7 -> x0, local copies, waits for them, and re-layouts: 11.4 us -> none
    pallas_call x3 -> x0, local copies, waits for them, and re-layouts: 4.35 us -> none  [shards(): pl.pallas_call(kernel, out_shape=outs, in_specs=[in_any if i in (3, 5, 7,...]
where the time goes in v2:
time: 119 us; the launch traced here: 118 us
  Pallas kernels  118 us (99%)
    pallas_call x1, Pallas kernels, shards(): pl.pallas_call(kernel, out_shape=outs + [jax.ShapeDtypeStruct((32, CH), F...  116 us

profile of v2, /device:TPU:1, one launch (start us, length us, event | category | flops | bytes accessed | tf_op | source)
XLA Modules:
  0.0 118.5 jit_solution(14316146032114072544)
XLA Ops:
  0.6 116.0 %shard_map.198 = (bf16[128,256]{1,0:T(8,128)(2,1)}, bf16[32,128]{1,0:T(8,128)(2,1)}, bf16[32,128]{1,0:T(8,128)(2,1)}, bf16[128,256]{1,0:T(8,128)(2,1)}, bf16[128...) custom-call(bf16[128,512]{1,0:T(8,128)(2,1)} %tok.1, bf16[128,512]{1,0:T(8,128)(2,1)} %mix.1, ...), custom_call_target="tpu_custom_call" | custom-call | flops 4831838208 | bytes 12000000 | tf_op jit(solution)/shard_map/pallas_call | solution.py:564
  116.7 1.8 %shard_map.199 = (bf16[128,256]{1,0:T(8,128)(2,1)}, bf16[32,128]{1,0:T(8,128)(2,1)}, bf16[32,128]{1,0:T(8,128)(2,1)}, bf16[128,256]{1,0:T(8,128)(2,1)}, bf16[128...) custom-call(bf16[128,256]{1,0:T(8,128)(2,1)} %get-tuple-element.21.refs_0_, ...), custom_call_target="tpu_custom_call" | custom-call | tf_op jit(solution)/shard_map/pallas_call | solution.py:584

commit v3 on v2

--- a/solution.py
+++ b/solution.py
@@ -16,6 +16,7 @@
 SEC = 5
 ROWS = 576
 HALF = 288
+PARTS = (pl.ds(0, 320), pl.ds(320, 256))
 NT = (((1,), (1,)), ((), ()))
 
 
@@ -101,18 +102,18 @@
             device_id={axis: peer}, device_id_type=MESH,
         )
 
+    bar = pltpu.get_barrier_semaphore()
+    loop(1, N, lambda i: pl.semaphore_signal(
+        bar, inc=1, device_id={"tensor": lax.rem(t + i, N)}, device_id_type=MESH))
+    for peer in dp_peers:
+        pl.semaphore_signal(bar, inc=1, device_id={"dp": peer}, device_id_type=MESH)
+
     loads = [
         pltpu.make_async_copy(src, dst, ld.at[i])
         for i, (src, dst) in enumerate(((kp, packk), (vp, packv), (qp, packq), (op, packo)))
     ]
     for load in loads:
         load.start()
-    bar = pltpu.get_barrier_semaphore()
-    loop(1, N, lambda i: pl.semaphore_signal(
-        bar, inc=1, device_id={"tensor": lax.rem(t + i, N)}, device_id_type=MESH))
-    for peer in dp_peers:
-        pl.semaphore_signal(bar, inc=1, device_id={"dp": peer}, device_id_type=MESH)
-
     r = lax.broadcasted_iota(jnp.int32, (CH, CH), 0)
     col = lax.broadcasted_iota(jnp.int32, (CH, CH), 1)
     perm[...] = jnp.where(col == 4 * (r & 127) + (r >> 7), 1.0, 0.0).astype(BF16)
@@ -120,41 +121,9 @@
     tok_t[1] = dot_nt(perm[...], mix[...]).astype(BF16)
     own = c * 16 + x * 4 + z
     ag[own, 0:256, :] = dot_nt(eye(256), qc[...]).astype(BF16)
-    ag[own, 256:512, :] = dot_nt(eye(256), oc[...]).astype(BF16)
-    ag[own, 512:544, :] = kc[...]
-    ag[own, 544:576, :] = vc[...]
-    pl.semaphore_wait(bar, N - 1 + 4)
-
-    def mine(p):
-        return pl.ds(pl.multiple_of(p * SUB, SUB), SUB)
-
-    def in_copy(p, slot):
-        return send(tok_t.at[:, mine(p), :], hin.at[slot], s1.at[p], r1.at[slot], p)
-
-    loop(1, N, lambda i: in_copy(lax.rem(t + i, N), t).start())
-    hin[t] = tok_t[:, mine(t), :]
-
-    def ag_copy(k, x_, z_, peer, sems):
-        slot = c * 16 + x_ * 4 + z_
-        return send(ag.at[slot], ag.at[slot], ag_s.at[k], sems.at[x_ * 4 + z_], peer)
-
-    def ag_wait(x_, z_, sems):
-        slot = c * 16 + x_ * 4 + z_
-        send(ag.at[slot], ag.at[slot], ag_s.at[0], sems.at[x_ * 4 + z_], sib).wait_recv()
-
-    def zrel(dz):
-        return lax.rem(z + dz, 4)
-
-    for dz in (1, 2, 3):
-        ag_copy(dz - 1, x, z, dev(x, zrel(dz), c), ag_r).start()
-
-    def ag_row(dz):
-        ag_copy(3 + 2 * dz, x, zrel(dz), dev(xp, z, c), ag_r).start()
-        ag_copy(4 + 2 * dz, x, zrel(dz), dev(xm, z, c), ag_r).start()
-        ag_copy(15 + dz, x, zrel(dz), sib, ag_sib).start()
-
-    ag_row(0)
-
+    ag[own, 320:576, :] = dot_nt(eye(256), oc[...]).astype(BF16)
+    ag[own, 256:288, :] = kc[...]
+    ag[own, 288:320, :] = vc[...]
     lanes = lax.broadcasted_iota(jnp.int32, (SUB, TOK), 1)
     subs = lax.broadcasted_iota(jnp.int32, (SUB, TOK), 0)
     pick = lanes == 4 * subs + (64 * c + x)
@@ -177,11 +146,106 @@
     loads[1].wait()
     dequantize(packv, vs, wv, 0, 1024)
 
-    def wait_in(i):
-        p = lax.rem(t + i, N)
-        in_copy(p, p).wait_recv()
-
-    loop(1, N, wait_in)
+    pl.semaphore_wait(bar, N - 1 + 4)
+
+    def mine(p):
+        return pl.ds(pl.multiple_of(p * SUB, SUB), SUB)
+
+    def group(ref, ssem, rsem, k=0):
+        all_ = ref.at[pl.ds(0, N - 1)]
+        return send(all_, all_, ssem.at[k], rsem.at[k], sib)
+
+    def in_copy(p, slot):
+        return send(tok_t.at[:, mine(p), :], hin.at[slot], s1.at[0], r1.at[0], p)
+
+    near = z - 1 + 2 * lax.div(3 - z, 3)
+    last = 3 * (1 - lax.div(z, 2))
+    order = (z, near, 6 - z - near - last, last)
+
+    def ag_copy(k, part_, x_, z_, peer, sems):
+        here = ag.at[c * 16 + x_ * 4 + z_, PARTS[part_], :]
+        at = part_ * 16 + x_ * 4 + z_
+        return send(here, here, ag_s.at[part_ * 33 + k], sems.at[at], peer)
+
+    def ag_wait(part_, x_, z_):
+        ag_copy(0, part_, x_, z_, sib, ag_r).wait_recv()
+
+    def upward(part_, k, z_):
+        return ag_copy(k, part_, x, z_, dev(x, z + 1, c), ag_r)
+
+    def downward(part_, k, z_):
+        return ag_copy(k, part_, x, z_, dev(x, z - 1, c), ag_r)
+
+    def ag_z(part_, act):
+        @pl.when(z < 3)
+        def _():
+            act(upward(part_, 0, z))
+
+        @pl.when(z > 0)
+        def _():
+            act(downward(part_, 1, z))
+
+    def ag_on(part_, k, act):
+        @pl.when((order[k] < z) & (z < 3))
+        def _():
+            act(upward(part_, 1 + k, order[k]))
+
+        @pl.when((order[k] > z) & (z > 0))
+        def _():
+            act(downward(part_, 1 + k, order[k]))
+
+    def start(copy):
+        copy.start()
+
+    def left(copy):
+        copy.wait_send()
+
+    def ag_row(part_, k):
+        ag_copy(5 + 2 * k, part_, x, order[k], dev(xp, z, c), ag_r).start()
+        ag_copy(6 + 2 * k, part_, x, order[k], dev(xm, z, c), ag_r).start()
+        ag_copy(17 + k, part_, x, order[k], sib, ag_sib).start()
+
+    def ag_col(part_, k):
+        ag_wait(part_, x, order[k])
+        ag_on(part_, k, start)
+        ag_row(part_, k)
+
+    def ag_near(part_, k):
+        ag_wait(part_, xm, order[k])
+        if k % 2 == 0:
+            ag_copy(13 + k, part_, xm, order[k], dev(xp, z, c), ag_r).start()
+        ag_copy(21 + k, part_, xm, order[k], sib, ag_sib).start()
+        ag_wait(part_, xp, order[k])
+        if k % 2 == 1:
+            ag_copy(13 + k, part_, xp, order[k], dev(xm, z, c), ag_r).start()
+        ag_copy(25 + k, part_, xp, order[k], sib, ag_sib).start()
+
+    def ag_far(part_, k):
+        ag_wait(part_, x2, order[k])
+        ag_copy(29 + k, part_, x2, order[k], sib, ag_sib).start()
+
+    def ag_own(part_):
+        for x_ in range(4):
+            for z_ in range(4):
+                here = ag.at[(1 - c) * 16 + x_ * 4 + z_, PARTS[part_], :]
+                at = part_ * 16 + x_ * 4 + z_
+                send(here, here, ag_s.at[0], ag_sib.at[at], sib).wait_recv()
+
+    ag_z(0, start)
+    ag_row(0, 0)
+    loop(1, N, lambda i: in_copy(lax.rem(t + i, N), t).start())
+    hin[t] = tok_t[:, mine(t), :]
+    ag_z(1, start)
+    ag_row(1, 0)
+
+    loads[2].wait()
+    dequantize(packq, qs, wq, 0, 2048)
+    ag_col(0, 1)
+    dequantize(packq, qs, wq, 2048, 2048)
+    ag_near(0, 0)
+    ag_col(0, 2)
+
+    group(hin, s1, r1).wait_recv()
 
     def pair_of(n, pr):
         sh = 4 - n
@@ -212,34 +276,26 @@
         loop(0, 16, forward)
 
     def h5_copy(p, src):
-        return send(h5s.at[p], h5t.at[:, mine(src), :], s2.at[p], r2.at[src], p)
+        return send(h5s.at[p], h5t.at[:, mine(src), :], s2.at[0], r2.at[0], p)
 
     loop(1, N, lambda i: h5_copy(lax.rem(t + i, N), t).start())
     h5t[:, mine(t), :] = h5s[t]
 
-    for dz in (1, 3, 2):
-        ag_wait(x, zrel(dz), ag_r)
-        ag_row(dz)
-    loads[2].wait()
-    for dz in range(4):
-        dequantize(packq, qs, wq, 2048 * dz, 2048)
-        ag_wait(xm, zrel(dz), ag_r)
-        if dz % 2 == 0:
-            ag_copy(11 + dz // 2, xm, zrel(dz), dev(xp, z, c), ag_r).start()
-        ag_copy(19 + dz, xm, zrel(dz), sib, ag_sib).start()
-        ag_wait(xp, zrel(dz), ag_r)
-        if dz % 2 == 1:
-            ag_copy(13 + dz // 2, xp, zrel(dz), dev(xm, z, c), ag_r).start()
-        ag_copy(23 + dz, xp, zrel(dz), sib, ag_sib).start()
-    loads[3].wait()
-    for dz in range(4):
-        dequantize(packo, os_, wo, 2048 * dz, 2048)
-        ag_wait(x2, zrel(dz), ag_r)
-        ag_copy(27 + dz, x2, zrel(dz), sib, ag_sib).start()
-
-    def wait_h5(i):
-        p = lax.rem(t + i, N)
-        h5_copy(p, p).wait_recv()
+    ag_col(0, 3)
+    ag_col(1, 1)
+    ag_near(0, 1)
+    dequantize(packq, qs, wq, 4096, 2048)
+    ag_col(1, 2)
+    ag_near(0, 2)
+    ag_near(1, 0)
+    dequantize(packq, qs, wq, 6144, 2048)
+    ag_near(0, 3)
+    ag_far(0, 0)
+    ag_col(1, 3)
+    ag_far(0, 1)
+    ag_far(0, 2)
+    ag_near(1, 1)
+    ag_far(0, 3)
 
     def narrow(j, w, first):
         piece = dot(hl[j], w[...]).astype(BF16)
@@ -252,7 +308,7 @@
     def wide(zp):
         def column(x_):
             cols = pl.ds(pl.multiple_of((x_ * 4 + zp) * 512, 512), 512)
-            for j, w, first in ((0, wq, 0), (3, wo, 256)):
+            for j, w, first in ((0, wq, 0), (3, wo, 320)):
                 piece = dot(hl[j], w[:, cols]).astype(BF16)
                 for c_ in range(2):
                     for half in range(2):
@@ -263,7 +319,7 @@
         loop(0, 4, column)
 
     def piece_z(p):
-        return lax.rem(z + 1 + p, 4)
+        return (3, 0, 2, 1)[p]
 
     def base(zp):
         return (c * 4 + zp) * 4
@@ -290,9 +346,13 @@
             rx2_s.at[2 * p + way], rx2_r.at[2 * p + way], dev(to, z, c),
         )
 
-    def z_copy(p, src):
-        zp = piece_z(p)
-        return send(accx.at[zp], rz.at[src], rz_s.at[p], rz_r.at[src], dev(x, zp, c))
+    def z_copy(dest, src):
+        return send(
+            accx.at[dest], rz.at[src], rz_s.at[dest], rz_r.at[src], dev(x, dest, c)
+        )
+
+    def stage_z(dest):
+        pl.when(z != dest)(lambda: z_copy(dest, z).start())
 
     def stage_x1(p):
         zp = piece_z(p)
@@ -317,15 +377,6 @@
         x2_copy(p, 0).wait_recv()
         x2_copy(p, 1).wait_recv()
         add_rows(part, base(zp) + x, (0, ROWS), [(rx2, (zp, 0), 0), (rx2, (zp, 1), 0)], accx, zp)
-        if p < 3:
-            z_copy(p, z).start()
-
-    for x_ in range(4):
-        for z_ in range(4):
-            slot = (1 - c) * 16 + x_ * 4 + z_
-            send(
-                ag.at[slot], ag.at[slot], ag_s.at[0], ag_sib.at[x_ * 4 + z_], sib
-            ).wait_recv()
 
     def back_wide(j, w, first):
         total = None
@@ -355,73 +406,88 @@
     def back_copy(k, p, slot):
         js = pl.ds(0, 3) if k == 0 else pl.ds(3, 1)
         return send(
-            bks.at[js, mine(p), :], bkr.at[slot, js], s3.at[k * N + p], r3.at[k * N + slot], p
+            bks.at[js, mine(p), :], bkr.at[slot, js], s3.at[k], r3.at[k], p
         )
 
+    ag_own(0)
     back_wide(0, wq, 0)
-    back_narrow(1, wk, 512)
-    back_narrow(2, wv, 544)
+    back_narrow(1, wk, 256)
+    back_narrow(2, wv, 288)
     loop(1, N, lambda i: back_copy(0, lax.rem(t + i, N), t).start())
-    back_wide(3, wo, 256)
-    loop(1, N, lambda i: back_copy(1, lax.rem(t + i, N), t).start())
-    bkr[t] = bks[:, mine(t), :]
-
-    loop(1, N, wait_h5)
+    bkr[t, 0:3] = bks[0:3, mine(t), :]
+    loads[3].wait()
+    dequantize(packo, os_, wo, 0, 4096)
+    ag_near(1, 2)
+    ag_near(1, 3)
+    ag_far(1, 0)
+    dequantize(packo, os_, wo, 4096, 4096)
+
+    group(h5s, s2, r2).wait_recv()
     for j in range(4):
         hl[j] = dot_nt(eye(TOK), h5t[j]).astype(BF16)
-    narrow(1, wk, 512)
-    narrow(2, wv, 544)
-    for p in range(4):
-        wide(piece_z(p))
-        a_copy(p).start()
-        if p:
-            stage_x1(p - 1)
+    narrow(1, wk, 256)
+    narrow(2, wv, 288)
+    wide(piece_z(0))
+    a_copy(0).start()
+    wide(piece_z(1))
+    a_copy(1).start()
+    stage_x1(0)
+    for k in (1, 2, 3):
+        ag_far(1, k)
+    ag_own(1)
+    back_wide(3, wo, 320)
+    loop(1, N, lambda i: back_copy(1, lax.rem(t + i, N), t).start())
+    bkr[t, 3] = bks[3, mine(t), :]
+    wide(piece_z(2))
+    a_copy(2).start()
+    stage_x1(1)
+    stage_x2(0)
+    wide(piece_z(3))
+    a_copy(3).start()
+    stage_x1(2)
+    stage_x2(1)
+
+    def backward_sections(js):
+        for n in reversed(range(SEC)):
+            take, put = (bkr, gb) if n % 2 == 0 else (gb, bkr)
+
+            def backward(pr, grads, n=n, take=take, put=put):
+                t0, t1 = pair_of(n, pr)
+                lows, highs = [], []
+                for j in js:
+                    cs, sn = ccos[n, pr, j], csin[n, pr, j]
+                    gl, gu = take[t0, j].astype(F32), take[t1, j].astype(F32)
+                    low = cs * gl + sn * gu
+                    high = cs * gu - sn * gl
+                    e = state(n, t0, j) * high - state(n, t1, j) * low
+                    total = jnp.sum(e, axis=1, keepdims=True) * (1.0 + cs)
+                    grads = jnp.where(lanes == pr * 4 + j, total, grads)
+                    lows.append(low)
+                    highs.append(high)
+                    if n:
+                        put[t0, j] = low.astype(BF16)
+                        put[t1, j] = high.astype(BF16)
+                if n == 0:
+                    for blk, parts in ((t0, lows), (t1, highs)):
+                        whole = parts[0] + parts[1] + parts[2] if len(js) == 3 else parts[0]
+                        gs[0 if len(js) == 3 else 1, blk] = whole.astype(BF16)
+                return grads
+
+            first = jnp.zeros((SUB, TOK), F32) if len(js) == 3 else angy[y, n]
+            angy[y, n] = lax.fori_loop(0, 16, backward, first, unroll=BU)
+
+    def out_copy(k, p, src):
+        return send(gs.at[k, p], gt.at[k, mine(src), :], s4.at[k], r4.at[k], p)
+
+    group(bkr.at[:, pl.ds(0, 3)], s3, r3).wait_recv()
+    backward_sections((0, 1, 2))
+    loop(1, N, lambda i: out_copy(0, lax.rem(t + i, N), t).start())
     stage_x1(3)
-    stage_x2(0)
-    stage_x2(1)
+    stage_x2(2)
     stage_x3(0)
-
-    def wait_back(i):
-        p = lax.rem(t + i, N)
-        back_copy(0, p, p).wait_recv()
-        back_copy(1, p, p).wait_recv()
-
-    loop(1, N, wait_back)
-
-    for n in reversed(range(SEC)):
-        take, put = (bkr, gb) if n % 2 == 0 else (gb, bkr)
-
-        def backward(pr, grads, n=n, take=take, put=put):
-            t0, t1 = pair_of(n, pr)
-            lows, highs = [], []
-            for j in range(4):
-                cs, sn = ccos[n, pr, j], csin[n, pr, j]
-                gl, gu = take[t0, j].astype(F32), take[t1, j].astype(F32)
-                low = cs * gl + sn * gu
-                high = cs * gu - sn * gl
-                e = state(n, t0, j) * high - state(n, t1, j) * low
-                total = jnp.sum(e, axis=1, keepdims=True) * (1.0 + cs)
-                grads = jnp.where(lanes == pr * 4 + j, total, grads)
-                lows.append(low)
-                highs.append(high)
-                if n:
-                    put[t0, j] = low.astype(BF16)
-                    put[t1, j] = high.astype(BF16)
-            if n == 0:
-                for blk, parts in ((t0, lows), (t1, highs)):
-                    gs[blk, 0] = (parts[0] + parts[1] + parts[2]).astype(BF16)
-                    gs[blk, 1] = parts[3].astype(BF16)
-            return grads
-
-        angy[y, n] = lax.fori_loop(0, 16, backward, jnp.zeros((SUB, TOK), F32), unroll=BU)
-        if n == 4:
-            stage_x2(2)
-        elif n == 3:
-            stage_x3(1)
-        elif n == 2:
-            stage_x2(3)
-        elif n == 1:
-            stage_x3(2)
+    stage_z(piece_z(0))
+    group(bkr.at[:, pl.ds(3, 1)], s3, r3, 1).wait_recv()
+    backward_sections((3,))
 
     def y_copy(k, slot):
         return send(angy.at[slot], angy.at[slot], sd.at[k], rd.at[slot], dp_peers[k], "dp")
@@ -429,35 +495,25 @@
     for k in range(3):
         y_copy(k, y).start()
 
-    def out_copy(p, src):
-        return send(gs.at[p], gt.at[:, mine(src), :], s4.at[p], r4.at[src], p)
-
-    loop(1, N, lambda i: out_copy(lax.rem(t + i, N), t).start())
-    gt[:, mine(t), :] = gs[t]
-    stage_x3(3)
+    loop(1, N, lambda i: out_copy(1, lax.rem(t + i, N), t).start())
+    for k in range(2):
+        gt[k, mine(t), :] = gs[k, t]
+    stage_x2(3)
+    stage_x3(1)
+    stage_z(piece_z(1))
+
+    def far_copy(slot):
+        return send(angz.at[slot], angz.at[slot], sd.at[3], rd.at[4], far, "dp")
+
     for k in range(3):
         y_copy(k, lax.rem(y + 1 + k, 4)).wait_recv()
     for n in range(SEC):
         angz[zh, n] = ((angy[0, n] + angy[1, n]) + angy[2, n]) + angy[3, n]
-
-    def far_copy(slot):
-        return send(angz.at[slot], angz.at[slot], sd.at[3], rd.at[4], far, "dp")
-
     far_copy(zh).start()
-
-    for p in range(3):
-        src = lax.rem(z + 1 + p, 4)
-        z_copy(0, src).wait_recv()
-    total = accx[z].astype(F32)
-    for p in range(3):
-        total = total + rz[lax.rem(z + 1 + p, 4)].astype(F32)
-    total = total.astype(BF16)
-    q_out[:, 0:128] = total[0:128]
-    q_out[:, 128:256] = total[128:256]
-    o_out[:, 0:128] = total[256:384]
-    o_out[:, 128:256] = total[384:512]
-    k_out[...] = total[512:544]
-    v_out[...] = total[544:576]
+    stage_x3(2)
+    stage_z(piece_z(2))
+    stage_x3(3)
+    stage_z(piece_z(3))
 
     far_copy(1 - zh).wait_recv()
     for n in range(SEC):
@@ -477,50 +533,55 @@
         angs[blk] = jnp.where(lanes < 32, top, rest).astype(BF16)
 
     def ang_copy(p, src):
-        return send(angs.at[p], angt.at[mine(src), :], s5.at[p], r5.at[src], p)
+        return send(angs.at[p], angt.at[mine(src), :], s5.at[0], r5.at[0], p)
 
     loop(0, N, message, unroll=4)
     loop(1, N, lambda i: ang_copy(lax.rem(t + i, N), t).start())
     angt[mine(t), :] = angs[t]
 
-    def wait_out(i):
-        p = lax.rem(t + i, N)
-        out_copy(p, p).wait_recv()
-
-    loop(1, N, wait_out)
+    total = accx[z].astype(F32)
+    for k in (1, 2, 3):
+        z_copy(0, order[k]).wait_recv()
+    for k in (1, 2, 3):
+        total = total + rz[order[k]].astype(F32)
+    total = total.astype(BF16)
+    q_out[:, 0:128] = total[0:128]
+    q_out[:, 128:256] = total[128:256]
+    o_out[:, 0:128] = total[320:448]
+    o_out[:, 128:256] = total[448:576]
+    k_out[...] = total[256:288]
+    v_out[...] = total[288:320]
 
     def natural(value):
         return dot(dot_nt(eye(TOK), value).astype(BF16), perm[...])
 
+    group(gs.at[0], s4, r4).wait_recv()
     tg[...] = natural(gt[0]).astype(BF16)
+    group(gs.at[1], s4, r4, 1).wait_recv()
     mg[...] = natural(gt[1]).astype(BF16)
 
-    def wait_ang(i):
-        p = lax.rem(t + i, N)
-        ang_copy(p, p).wait_recv()
-
-    loop(1, N, wait_ang)
+    group(angs, s5, r5).wait_recv()
     both = natural(angt[...])
     ang_out[...] = both[0:32] + both[32:64]
 
-    def drain(i):
-        p = lax.rem(t + i, N)
-        in_copy(p, t).wait_send()
-        h5_copy(p, t).wait_send()
-        back_copy(0, p, t).wait_send()
-        back_copy(1, p, t).wait_send()
-        ang_copy(p, t).wait_send()
-        out_copy(p, t).wait_send()
-
-    loop(1, N, drain)
-    loop(0, 31, lambda i: ag_copy(i, x, z, sib, ag_r).wait_send())
+    group(hin, s1, r1).wait_send()
+    group(h5s, s2, r2).wait_send()
+    group(bkr.at[:, pl.ds(0, 3)], s3, r3).wait_send()
+    group(bkr.at[:, pl.ds(3, 1)], s3, r3, 1).wait_send()
+    group(gs.at[0], s4, r4).wait_send()
+    group(gs.at[1], s4, r4, 1).wait_send()
+    group(angs, s5, r5).wait_send()
+    for part_ in range(2):
+        ag_z(part_, left)
+        for k in (1, 2, 3):
+            ag_on(part_, k, left)
+        loop(5, 33, lambda i, p=part_: ag_copy(i, p, x, z, sib, ag_r).wait_send())
     for p in range(4):
         a_copy(p).wait_send()
         for way in range(2):
             x1_copy(p, way).wait_send()
             x2_copy(p, way).wait_send()
-        if p < 3:
-            z_copy(p, z).wait_send()
+        pl.when(z != p)(lambda p=p: z_copy(p, z).wait_send())
     for k in range(3):
         y_copy(k, y).wait_send()
     far_copy(zh).wait_send()
@@ -547,12 +608,12 @@
         vm((4, ROWS, TOK)), vm((4, ROWS, TOK)),
         vm((CH, TOK), F32),
         vm((4, CH, TOK)), vm((N, 4, SUB, TOK)), vm((N, 4, SUB, TOK)),
-        vm((N, 2, SUB, TOK)), vm((2, CH, TOK)),
+        vm((2, N, SUB, TOK)), vm((2, CH, TOK)),
         vm((4, SEC, SUB, TOK), F32), vm((2, SEC, SUB, TOK), F32),
         vm((SEC, 16, SUB, TOK), F32), vm((N, SUB, TOK)), vm((CH, TOK)),
-        sem(4), sem(N), sem(N), sem(N), sem(N), sem(2 * N), sem(2 * N), sem(N), sem(N),
-        sem(31), sem(16), sem(16), sem(4), sem(4), sem(8), sem(8), sem(8), sem(8),
-        sem(4), sem(4), sem(4), sem(5), sem(N), sem(N),
+        sem(4), sem(1), sem(1), sem(1), sem(1), sem(2), sem(2), sem(2), sem(2),
+        sem(66), sem(32), sem(32), sem(4), sem(4), sem(8), sem(8), sem(8), sem(8),
+        sem(4), sem(4), sem(4), sem(5), sem(1), sem(1),
     ]
     shapes = [(TOK, 256), (32, TOK), (32, TOK), (TOK, 256), (TOK, CH), (TOK, CH)]
     outs = [jax.ShapeDtypeStruct(shape, BF16) for shape in shapes]

time: 119 us -> 103 us (0.87)
  Pallas kernels: 118 us -> 102 us
    pallas_call x1, Pallas kernels: 116 us -> 100 us  [shards(): pl.pallas_call(kernel, out_shape=outs + [jax.ShapeDtypeStruct((32, CH), F...]
where the time goes in v3:
time: 103 us
  Pallas kernels  102 us (99%)
    pallas_call x1, Pallas kernels, shards(): pl.pallas_call(kernel, out_shape=outs + [jax.ShapeDtypeStruct((32, CH), F...  100 us

profile of v3, /device:TPU:1, one launch (start us, length us, event | category | flops | bytes accessed | tf_op | source)
XLA Modules:
  0.0 102.8 jit_solution(14193266052590013448)
XLA Ops:
  0.6 100.3 %shard_map.198 = (bf16[128,256]{1,0:T(8,128)(2,1)}, bf16[32,128]{1,0:T(8,128)(2,1)}, bf16[32,128]{1,0:T(8,128)(2,1)}, bf16[128,256]{1,0:T(8,128)(2,1)}, bf16[128...) custom-call(bf16[128,512]{1,0:T(8,128)(2,1)} %tok.1, bf16[128,512]{1,0:T(8,128)(2,1)} %mix.1, ...), custom_call_target="tpu_custom_call" | custom-call | flops 4831838208 | bytes 12000000 | tf_op jit(solution)/shard_map/pallas_call | solution.py:625
  100.9 1.8 %shard_map.199 = (bf16[128,256]{1,0:T(8,128)(2,1)}, bf16[32,128]{1,0:T(8,128)(2,1)}, bf16[32,128]{1,0:T(8,128)(2,1)}, bf16[128,256]{1,0:T(8,128)(2,1)}, bf16[128...) custom-call(bf16[128,256]{1,0:T(8,128)(2,1)} %get-tuple-element.21.refs_0_, ...), custom_call_target="tpu_custom_call" | custom-call | tf_op jit(solution)/shard_map/pallas_call | solution.py:645

commit v4 on v3

--- a/solution.py
+++ b/solution.py
@@ -76,7 +76,7 @@
     tok, mix, ang, qp, qs, kp, ks, vp, vs, op, os_, qc, kc, vc, oc,
     q_out, k_out, v_out, o_out, tg, mg, ang_out,
     packq, packk, packv, packo, wq, wk, wv, wo, perm,
-    tok_t, hin, st, h5s, h5t, hl, ccos, csin,
+    angv, tok_t, hin, st, h5s, h5t, hl, ccos, csin,
     ag, part, ra, rx1, rx2, accx, rz, acc, bks, bkr, gb, gs, gt, angy, angz, spread, angs, angt,
     ld, s1, r1, s2, r2, s3, r3, s4, r4, ag_s, ag_r, ag_sib, ra_s, ra_r, rx1_s, rx1_r,
     rx2_s, rx2_r, rz_s, rz_r, sd, rd, s5, r5,
@@ -110,10 +110,10 @@
 
     loads = [
         pltpu.make_async_copy(src, dst, ld.at[i])
-        for i, (src, dst) in enumerate(((kp, packk), (vp, packv), (qp, packq), (op, packo)))
+        for i, (src, dst) in enumerate(((kp, packk), (vp, packv), (qp, packq), (op, packo), (ang, angv)))
     ]
-    for load in loads:
-        load.start()
+    for i in (4, 0, 1, 2, 3):
+        loads[i].start()
     r = lax.broadcasted_iota(jnp.int32, (CH, CH), 0)
     col = lax.broadcasted_iota(jnp.int32, (CH, CH), 1)
     perm[...] = jnp.where(col == 4 * (r & 127) + (r >> 7), 1.0, 0.0).astype(BF16)
@@ -124,28 +124,6 @@
     ag[own, 320:576, :] = dot_nt(eye(256), oc[...]).astype(BF16)
     ag[own, 256:288, :] = kc[...]
     ag[own, 288:320, :] = vc[...]
-    lanes = lax.broadcasted_iota(jnp.int32, (SUB, TOK), 1)
-    subs = lax.broadcasted_iota(jnp.int32, (SUB, TOK), 0)
-    pick = lanes == 4 * subs + (64 * c + x)
-    window = 128 * lax.div(lax.rem(t, 8), 2)
-
-    def factors(pr):
-        where = pl.ds(pl.multiple_of(pr * CH + window, 128), 128)
-        for j in range(4):
-            for n in range(SEC):
-                row = jnp.broadcast_to(ang[n, j : j + 1, where], (SUB, TOK))
-                angle = jnp.sum(jnp.where(pick, row, 0.0), axis=1, keepdims=True)
-                square = angle * angle
-                inverse = 1.0 / (1.0 + square)
-                ccos[n, pr, j] = jnp.broadcast_to((1.0 - square) * inverse, (SUB, TOK))
-                csin[n, pr, j] = jnp.broadcast_to(2.0 * angle * inverse, (SUB, TOK))
-
-    loop(0, 16, factors)
-    loads[0].wait()
-    dequantize(packk, ks, wk, 0, 1024)
-    loads[1].wait()
-    dequantize(packv, vs, wv, 0, 1024)
-
     pl.semaphore_wait(bar, N - 1 + 4)
 
     def mine(p):
@@ -237,6 +215,30 @@
     hin[t] = tok_t[:, mine(t), :]
     ag_z(1, start)
     ag_row(1, 0)
+
+    lanes = lax.broadcasted_iota(jnp.int32, (SUB, TOK), 1)
+    subs = lax.broadcasted_iota(jnp.int32, (SUB, TOK), 0)
+    pick = lanes == 4 * subs + (64 * c + x)
+    window = 128 * lax.div(lax.rem(t, 8), 2)
+
+    loads[4].wait()
+
+    def factors(pr):
+        where = pl.ds(pl.multiple_of(pr * CH + window, 128), 128)
+        for j in range(4):
+            for n in range(SEC):
+                row = jnp.broadcast_to(angv[n, j : j + 1, where], (SUB, TOK))
+                angle = jnp.sum(jnp.where(pick, row, 0.0), axis=1, keepdims=True)
+                square = angle * angle
+                inverse = 1.0 / (1.0 + square)
+                ccos[n, pr, j] = jnp.broadcast_to((1.0 - square) * inverse, (SUB, TOK))
+                csin[n, pr, j] = jnp.broadcast_to(2.0 * angle * inverse, (SUB, TOK))
+
+    loop(0, 16, factors)
+    loads[0].wait()
+    dequantize(packk, ks, wk, 0, 1024)
+    loads[1].wait()
+    dequantize(packv, vs, wv, 0, 1024)
 
     loads[2].wait()
     dequantize(packq, qs, wq, 0, 2048)
@@ -278,14 +280,14 @@
     def h5_copy(p, src):
         return send(h5s.at[p], h5t.at[:, mine(src), :], s2.at[0], r2.at[0], p)
 
-    loop(1, N, lambda i: h5_copy(lax.rem(t + i, N), t).start())
-    h5t[:, mine(t), :] = h5s[t]
 
     ag_col(0, 3)
     ag_col(1, 1)
     ag_near(0, 1)
     dequantize(packq, qs, wq, 4096, 2048)
     ag_col(1, 2)
+    loop(1, N, lambda i: h5_copy(lax.rem(t + i, N), t).start())
+    h5t[:, mine(t), :] = h5s[t]
     ag_near(0, 2)
     ag_near(1, 0)
     dequantize(packq, qs, wq, 6144, 2048)
@@ -434,13 +436,13 @@
     stage_x1(0)
     for k in (1, 2, 3):
         ag_far(1, k)
+    wide(piece_z(2))
+    a_copy(2).start()
+    stage_x1(1)
     ag_own(1)
     back_wide(3, wo, 320)
     loop(1, N, lambda i: back_copy(1, lax.rem(t + i, N), t).start())
     bkr[t, 3] = bks[3, mine(t), :]
-    wide(piece_z(2))
-    a_copy(2).start()
-    stage_x1(1)
     stage_x2(0)
     wide(piece_z(3))
     a_copy(3).start()
@@ -560,17 +562,12 @@
     group(gs.at[1], s4, r4, 1).wait_recv()
     mg[...] = natural(gt[1]).astype(BF16)
 
-    group(angs, s5, r5).wait_recv()
-    both = natural(angt[...])
-    ang_out[...] = both[0:32] + both[32:64]
-
     group(hin, s1, r1).wait_send()
     group(h5s, s2, r2).wait_send()
     group(bkr.at[:, pl.ds(0, 3)], s3, r3).wait_send()
     group(bkr.at[:, pl.ds(3, 1)], s3, r3, 1).wait_send()
     group(gs.at[0], s4, r4).wait_send()
     group(gs.at[1], s4, r4, 1).wait_send()
-    group(angs, s5, r5).wait_send()
     for part_ in range(2):
         ag_z(part_, left)
         for k in (1, 2, 3):
@@ -586,6 +583,11 @@
         y_copy(k, y).wait_send()
     far_copy(zh).wait_send()
 
+    group(angs, s5, r5).wait_recv()
+    both = dot(dot_nt(eye(TOK)[0:64], angt[...]).astype(BF16), perm[...])
+    ang_out[...] = both[0:32] + both[32:64]
+    group(angs, s5, r5).wait_send()
+
 
 def shards(*args):
     def vm(shape, dtype=BF16):
@@ -598,7 +600,7 @@
         vm((128, 8192), F32), vm((128, 1024), F32), vm((128, 1024), F32), vm((128, 8192), F32),
         vm((CH, 8192)), vm((CH, 1024)), vm((CH, 1024)), vm((CH, 8192)),
         vm((CH, CH)),
-        vm((2, CH, TOK)), vm((N, 2, SUB, TOK)),
+        vm((SEC, 4, 8192), F32), vm((2, CH, TOK)), vm((N, 2, SUB, TOK)),
         vm((SEC - 1, N, 4, SUB, TOK)), vm((N, 4, SUB, TOK)),
         vm((4, CH, TOK)), vm((4, TOK, CH)),
         vm((SEC, 16, 4, SUB, TOK), F32), vm((SEC, 16, 4, SUB, TOK), F32),
@@ -611,7 +613,7 @@
         vm((2, N, SUB, TOK)), vm((2, CH, TOK)),
         vm((4, SEC, SUB, TOK), F32), vm((2, SEC, SUB, TOK), F32),
         vm((SEC, 16, SUB, TOK), F32), vm((N, SUB, TOK)), vm((CH, TOK)),
-        sem(4), sem(1), sem(1), sem(1), sem(1), sem(2), sem(2), sem(2), sem(2),
+        sem(5), sem(1), sem(1), sem(1), sem(1), sem(2), sem(2), sem(2), sem(2),
         sem(66), sem(32), sem(32), sem(4), sem(4), sem(8), sem(8), sem(8), sem(8),
         sem(4), sem(4), sem(4), sem(5), sem(1), sem(1),
     ]
@@ -625,7 +627,7 @@
     results = pl.pallas_call(
         kernel,
         out_shape=outs + [jax.ShapeDtypeStruct((32, CH), F32)],
-        in_specs=[in_any if i in (3, 5, 7, 9) else in_vmem for i in range(15)],
+        in_specs=[in_any if i in (2, 3, 5, 7, 9) else in_vmem for i in range(15)],
         out_specs=[in_vmem] * 7,
         scratch_shapes=scratch,
         compiler_params=pltpu.CompilerParams(

time: 103 us -> 98.4 us (0.955)
  Pallas kernels: 102 us -> 97.7 us
    pallas_call x1, Pallas kernels: 100 us -> 95.8 us  [shards(): pl.pallas_call(kernel, out_shape=outs + [jax.ShapeDtypeStruct((32, CH), F...]
where the time goes in v4:
time: 98.4 us; the launch traced here: 98.3 us
  Pallas kernels  97.7 us (99%)
    pallas_call x1, Pallas kernels, shards(): pl.pallas_call(kernel, out_shape=outs + [jax.ShapeDtypeStruct((32, CH), F...  95.8 us

profile of v4, /device:TPU:1, one launch (start us, length us, event | category | flops | bytes accessed | tf_op | source)
XLA Modules:
  0.0 98.3 jit_solution(7816108538642911274)
XLA Ops:
  0.6 95.8 %shard_map.198 = (bf16[128,256]{1,0:T(8,128)(2,1)}, bf16[32,128]{1,0:T(8,128)(2,1)}, bf16[32,128]{1,0:T(8,128)(2,1)}, bf16[128,256]{1,0:T(8,128)(2,1)}, bf16[128...) custom-call(bf16[128,512]{1,0:T(8,128)(2,1)} %tok.1, bf16[128,512]{1,0:T(8,128)(2,1)} %mix.1, ...), custom_call_target="tpu_custom_call" | custom-call | flops 4831838208 | bytes 12000000 | tf_op jit(solution)/shard_map/pallas_call | solution.py:627
  96.5 1.8 %shard_map.199 = (bf16[128,256]{1,0:T(8,128)(2,1)}, bf16[32,128]{1,0:T(8,128)(2,1)}, bf16[32,128]{1,0:T(8,128)(2,1)}, bf16[128,256]{1,0:T(8,128)(2,1)}, bf16[128...) custom-call(bf16[128,256]{1,0:T(8,128)(2,1)} %get-tuple-element.21.refs_0_, ...), custom_call_target="tpu_custom_call" | custom-call | tf_op jit(solution)/shard_map/pallas_call | solution.py:647

commit v5 on v4

--- a/solution.py
+++ b/solution.py
@@ -283,11 +283,11 @@
 
     ag_col(0, 3)
     ag_col(1, 1)
+    loop(1, N, lambda i: h5_copy(lax.rem(t + i, N), t).start())
+    h5t[:, mine(t), :] = h5s[t]
     ag_near(0, 1)
     dequantize(packq, qs, wq, 4096, 2048)
     ag_col(1, 2)
-    loop(1, N, lambda i: h5_copy(lax.rem(t + i, N), t).start())
-    h5t[:, mine(t), :] = h5s[t]
     ag_near(0, 2)
     ag_near(1, 0)
     dequantize(packq, qs, wq, 6144, 2048)
@@ -507,13 +507,13 @@
     def far_copy(slot):
         return send(angz.at[slot], angz.at[slot], sd.at[3], rd.at[4], far, "dp")
 
+    stage_x3(2)
+    stage_z(piece_z(2))
     for k in range(3):
         y_copy(k, lax.rem(y + 1 + k, 4)).wait_recv()
     for n in range(SEC):
         angz[zh, n] = ((angy[0, n] + angy[1, n]) + angy[2, n]) + angy[3, n]
     far_copy(zh).start()
-    stage_x3(2)
-    stage_z(piece_z(2))
     stage_x3(3)
     stage_z(piece_z(3))
 

time: 98.4 us -> 99.2 us (level)
  no operation moved by 1% of the time
where the time goes in v5:
time: 99.2 us; the launch traced here: 99 us
  Pallas kernels  98.4 us (99%)
    pallas_call x1, Pallas kernels, shards(): pl.pallas_call(kernel, out_shape=outs + [jax.ShapeDtypeStruct((32, CH), F...  96.6 us

profile of v5, /device:TPU:1, one launch (start us, length us, event | category | flops | bytes accessed | tf_op | source)
XLA Modules:
  0.0 99.0 jit_solution(4282515910721135627)
XLA Ops:
  0.6 96.6 %shard_map.198 = (bf16[128,256]{1,0:T(8,128)(2,1)}, bf16[32,128]{1,0:T(8,128)(2,1)}, bf16[32,128]{1,0:T(8,128)(2,1)}, bf16[128,256]{1,0:T(8,128)(2,1)}, bf16[128...) custom-call(bf16[128,512]{1,0:T(8,128)(2,1)} %tok.1, bf16[128,512]{1,0:T(8,128)(2,1)} %mix.1, ...), custom_call_target="tpu_custom_call" | custom-call | flops 4831838208 | bytes 12000000 | tf_op jit(solution)/shard_map/pallas_call | solution.py:627
  97.2 1.8 %shard_map.199 = (bf16[128,256]{1,0:T(8,128)(2,1)}, bf16[32,128]{1,0:T(8,128)(2,1)}, bf16[32,128]{1,0:T(8,128)(2,1)}, bf16[128,256]{1,0:T(8,128)(2,1)}, bf16[128...) custom-call(bf16[128,256]{1,0:T(8,128)(2,1)} %get-tuple-element.21.refs_0_, ...), custom_call_target="tpu_custom_call" | custom-call | tf_op jit(solution)/shard_map/pallas_call | solution.py:647

commit v6 on v5

--- a/solution.py
+++ b/solution.py
@@ -9,7 +9,7 @@
 BF16 = jnp.bfloat16
 MESH = pl.DeviceIdType.MESH
 N = 32
-BU = 2
+BU = 4
 CH = 512
 SUB = 16
 TOK = 128
@@ -507,13 +507,13 @@
     def far_copy(slot):
         return send(angz.at[slot], angz.at[slot], sd.at[3], rd.at[4], far, "dp")
 
-    stage_x3(2)
-    stage_z(piece_z(2))
     for k in range(3):
         y_copy(k, lax.rem(y + 1 + k, 4)).wait_recv()
     for n in range(SEC):
         angz[zh, n] = ((angy[0, n] + angy[1, n]) + angy[2, n]) + angy[3, n]
     far_copy(zh).start()
+    stage_x3(2)
+    stage_z(piece_z(2))
     stage_x3(3)
     stage_z(piece_z(3))
 

time: 99.2 us -> 98.1 us (0.989)
  Pallas kernels: 98.4 us -> 97.4 us
    pallas_call x1, Pallas kernels: 96.6 us -> 95.5 us  [shards(): pl.pallas_call(kernel, out_shape=outs + [jax.ShapeDtypeStruct((32, CH), F...]
where the time goes in v6:
time: 98.1 us; the launch traced here: 98 us
  Pallas kernels  97.4 us (99%)
    pallas_call x1, Pallas kernels, shards(): pl.pallas_call(kernel, out_shape=outs + [jax.ShapeDtypeStruct((32, CH), F...  95.5 us

profile of v6, /device:TPU:1, one launch (start us, length us, event | category | flops | bytes accessed | tf_op | source)
XLA Modules:
  0.0 98.0 jit_solution(15620215771005818980)
XLA Ops:
  0.6 95.5 %shard_map.198 = (bf16[128,256]{1,0:T(8,128)(2,1)}, bf16[32,128]{1,0:T(8,128)(2,1)}, bf16[32,128]{1,0:T(8,128)(2,1)}, bf16[128,256]{1,0:T(8,128)(2,1)}, bf16[128...) custom-call(bf16[128,512]{1,0:T(8,128)(2,1)} %tok.1, bf16[128,512]{1,0:T(8,128)(2,1)} %mix.1, ...), custom_call_target="tpu_custom_call" | custom-call | flops 4831838208 | bytes 12000000 | tf_op jit(solution)/shard_map/pallas_call | solution.py:627
  96.2 1.8 %shard_map.199 = (bf16[128,256]{1,0:T(8,128)(2,1)}, bf16[32,128]{1,0:T(8,128)(2,1)}, bf16[32,128]{1,0:T(8,128)(2,1)}, bf16[128,256]{1,0:T(8,128)(2,1)}, bf16[128...) custom-call(bf16[128,256]{1,0:T(8,128)(2,1)} %get-tuple-element.21.refs_0_, ...), custom_call_target="tpu_custom_call" | custom-call | tf_op jit(solution)/shard_map/pallas_call | solution.py:647
